TPU v7x, 32 devices: a whole 2x2x4 slice. The times are simulated.
32 devices in a mesh: dp: 16 (over z, x, core), tensor: 2 (over y).
Axes of the slice: x: 2, y: 2, z: 4, core: 2. Of those that a mesh axis runs over, the one named last changes fastest.
Arguments:
- inputs: bfloat16 [16384, 1024], P('dp'), may hold values from -6 to 6
- lengths: int32 [16], P('dp'), may hold values from 256 to 1024, as said below
- gain_attn: bfloat16 [1024], replicated, may hold values from 0.5 to 1.5
- w_query: bfloat16 [1024, 1024], P(None, 'tensor'), may hold values from -0.1875 to 0.1875
- w_key: bfloat16 [1024, 1024], P(None, 'tensor'), may hold values from -0.1875 to 0.1875
- w_value: bfloat16 [1024, 1024], P(None, 'tensor'), may hold values from -0.1875 to 0.1875
- w_gate_attn: bfloat16 [1024, 1024], P(None, 'tensor'), may hold values from -0.1875 to 0.1875
- w_out: bfloat16 [1024, 1024], P('tensor'), may hold values from -0.25 to 0.25
- gain_ffn: bfloat16 [1024], replicated, may hold values from 0.5 to 1.5
- w_gate: bfloat16 [1024, 2816], P(None, 'tensor'), may hold values from -0.1875 to 0.1875
- w_up: bfloat16 [1024, 2816], P(None, 'tensor'), may hold values from -0.1875 to 0.1875
- w_down: bfloat16 [2816, 1024], P('tensor'), may hold values from -0.15625 to 0.15625
- cotangent: bfloat16 [16384, 1024], P('dp'), may hold values from -6 to 6
Outputs:
- result: bfloat16 [16384, 1024], P('dp')
- input_grad: bfloat16 [16384, 1024], P('dp')
- grad_gain_attn: float32 [1024], P('dp')
- grad_query: float32 [1024, 1024], P('dp', 'tensor')
- grad_key: float32 [1024, 1024], P('dp', 'tensor')
- grad_value: float32 [1024, 1024], P('dp', 'tensor')
- grad_gate_attn: float32 [1024, 1024], P('dp', 'tensor')
- grad_out: float32 [1024, 1024], P('tensor', 'dp')
- grad_gain_ffn: float32 [1024], P('dp')
- grad_gate: float32 [1024, 2816], P('dp', 'tensor')
- grad_up: float32 [1024, 2816], P('dp', 'tensor')
- grad_down: float32 [2816, 1024], P('tensor', 'dp')
Inputs may be any that keep to these rules, and one draw needn't show every extreme that they name: Each sequence occupies 1024 slots of which its first lengths are live; some sequence fills all 1024.
All inputs are finite; a program needn't handle non-finite values.
Results may differ from a plain program's by a relative error of at most 0.02.
Values sent between devices are 32-bit elements; how exact they have to be, the bound alone decides.
No kernel may reach another device: no remote copies, remote signals or barrier semaphores. Data moves between devices by JAX's collectives and lax.ppermute only.
A program may use at most 256 MiB of HBM per device.

v0:
```python
import jax
import jax.numpy as jnp
from jax import lax
from jax.sharding import PartitionSpec as P

HEADS = 16
HEAD_DIM = 64
BLOCK = 512


EPS = 1e-06
HIGHEST = lax.Precision.HIGHEST


def matmul(left, right):
    return jnp.dot(left, right, preferred_element_type=jnp.float32)


def inner_rows(left, right):
    return lax.dot_general(
        left, right, (((0,), (0,)), ((), ())), preferred_element_type=jnp.float32
    )


def times_transpose(left, right):
    return lax.dot_general(
        left, right, (((1,), (1,)), ((), ())), preferred_element_type=jnp.float32
    )


def silu_slope(value):
    logistic = jax.nn.sigmoid(value)
    return logistic * (1.0 + value * (1.0 - logistic))


def decay_tables(rates, block):
    offset = jnp.arange(block, dtype=jnp.float32)
    spread = offset[:, None] - offset[None, :]
    causal = (spread >= 0.0).astype(jnp.float32)
    within = jnp.exp(-rates[:, None, None] * (spread * causal)[None]) * causal[None]
    query_decay = jnp.exp(-rates[:, None] * (offset + 1.0)[None]).T[:, :, None]
    key_decay = jnp.exp(-rates[:, None] * (block - 1.0 - offset)[None]).T[:, :, None]
    block_decay = jnp.exp(-rates * block)[:, None, None]
    return (within, query_decay, key_decay, block_decay)


def row_norm_back(grad_normed, normed, scale, axis):
    return scale * (grad_normed - normed * jnp.mean(grad_normed * normed, axis=axis, keepdims=True))


def shards(
    inputs,
    lengths,
    gain_attn,
    w_query,
    w_key,
    w_value,
    w_gate_attn,
    w_out,
    gain_ffn,
    w_gate,
    w_up,
    w_down,
    cotangent,
):
    seq_rows = inputs.shape[0]
    local_heads = w_query.shape[1] // HEAD_DIM
    blocks = seq_rows // BLOCK
    shape_heads = (seq_rows, local_heads, HEAD_DIM)
    residual_in = inputs.astype(jnp.float32)
    positions = jnp.arange(seq_rows, dtype=jnp.int32)
    live = (positions < lengths[0]).astype(jnp.float32)[:, None]
    gain_one = gain_attn.astype(jnp.float32)
    gain_two = gain_ffn.astype(jnp.float32)
    scale_one = lax.rsqrt(jnp.mean(residual_in * residual_in, axis=1, keepdims=True) + EPS)
    normed_one = residual_in * scale_one
    hidden_one = (normed_one * gain_one).astype(jnp.bfloat16)
    query_pre = matmul(hidden_one, w_query)
    key_pre = matmul(hidden_one, w_key)
    query_round = jax.nn.softplus(query_pre).astype(jnp.bfloat16)
    key_round = (jax.nn.softplus(key_pre) * live).astype(jnp.bfloat16)
    value_round = matmul(hidden_one, w_value).astype(jnp.bfloat16)
    gate_attn = jax.nn.sigmoid(matmul(hidden_one, w_gate_attn))
    head_ids = (lax.axis_index("tensor") * local_heads + jnp.arange(local_heads)).astype(
        jnp.float32
    )
    rates = jnp.exp2(-8.0 * (head_ids + 1.0) / HEADS)
    within, query_decay, key_decay, block_decay = decay_tables(rates, BLOCK)
    queries = query_round.reshape(shape_heads)
    keys_all = key_round.reshape(shape_heads)
    values_all = value_round.reshape(shape_heads)
    state = jnp.zeros((local_heads, HEAD_DIM, HEAD_DIM), jnp.float32)
    states = []
    block_outputs = []
    for block_index in range(blocks):
        lower = block_index * BLOCK
        query_block = queries[lower : lower + BLOCK]
        key_block = keys_all[lower : lower + BLOCK]
        value_block = values_all[lower : lower + BLOCK]
        scores = jnp.einsum(
            "ihd,jhd->hij", query_block, key_block, preferred_element_type=jnp.float32
        )
        weights = (scores * within).astype(jnp.bfloat16)
        local_part = jnp.einsum(
            "hij,jhd->ihd", weights, value_block, preferred_element_type=jnp.float32
        )
        carried = (
            jnp.einsum("ihd,hde->ihe", query_block.astype(jnp.float32), state, precision=HIGHEST)
            * query_decay
        )
        block_outputs.append(local_part + carried)
        states.append(state)
        state = block_decay * state + jnp.einsum(
            "jhd,jhe->hde",
            key_block.astype(jnp.float32) * key_decay,
            value_block.astype(jnp.float32),
            precision=HIGHEST,
        )
    attended = jnp.concatenate(block_outputs, axis=0)
    scale_out = lax.rsqrt(jnp.mean(attended * attended, axis=2, keepdims=True) + EPS)
    normed_out = attended * scale_out
    gate_heads = gate_attn.reshape(shape_heads)
    mixed_round = (normed_out * gate_heads).reshape(seq_rows, -1).astype(jnp.bfloat16)
    attn_branch = lax.psum(matmul(mixed_round, w_out), "tensor")
    residual_mid = residual_in + live * attn_branch
    scale_two = lax.rsqrt(jnp.mean(residual_mid * residual_mid, axis=1, keepdims=True) + EPS)
    normed_two = residual_mid * scale_two
    hidden_two = (normed_two * gain_two).astype(jnp.bfloat16)
    gate_pre = matmul(hidden_two, w_gate)
    up_pre = matmul(hidden_two, w_up)
    gate_act = jax.nn.silu(gate_pre)
    glu_round = (gate_act * up_pre).astype(jnp.bfloat16)
    ffn_branch = lax.psum(matmul(glu_round, w_down), "tensor")
    result = (residual_mid + live * ffn_branch).astype(jnp.bfloat16)
    upstream = cotangent.astype(jnp.float32)
    ffn_out_grad = (live * upstream).astype(jnp.bfloat16)
    grad_down = inner_rows(glu_round, ffn_out_grad)
    glu_grad = times_transpose(ffn_out_grad, w_down)
    up_grad = (glu_grad * gate_act).astype(jnp.bfloat16)
    gate_grad = (glu_grad * up_pre * silu_slope(gate_pre)).astype(jnp.bfloat16)
    grad_gate = inner_rows(hidden_two, gate_grad)
    grad_up = inner_rows(hidden_two, up_grad)
    hidden_two_grad = lax.psum(
        times_transpose(gate_grad, w_gate) + times_transpose(up_grad, w_up), "tensor"
    )
    grad_gain_two = jnp.sum(hidden_two_grad * normed_two, axis=0)
    mid_grad = upstream + row_norm_back(hidden_two_grad * gain_two, normed_two, scale_two, 1)
    attn_out_grad = (live * mid_grad).astype(jnp.bfloat16)
    grad_out = inner_rows(mixed_round, attn_out_grad)
    mixed_grad = times_transpose(attn_out_grad, w_out).reshape(shape_heads)
    gate_pre_grad = (mixed_grad * normed_out).reshape(seq_rows, -1)
    gate_pre_grad = (gate_pre_grad * gate_attn * (1.0 - gate_attn)).astype(jnp.bfloat16)
    attended_grad = row_norm_back(mixed_grad * gate_heads, normed_out, scale_out, 2).astype(
        jnp.bfloat16
    )
    carry = jnp.zeros((local_heads, HEAD_DIM, HEAD_DIM), jnp.float32)
    query_parts = [None] * blocks
    key_parts = [None] * blocks
    value_parts = [None] * blocks
    for block_index in reversed(range(blocks)):
        lower = block_index * BLOCK
        query_block = queries[lower : lower + BLOCK]
        key_block = keys_all[lower : lower + BLOCK]
        value_block = values_all[lower : lower + BLOCK]
        out_grad_block = attended_grad[lower : lower + BLOCK]
        state = states[block_index]
        scores = jnp.einsum(
            "ihd,jhd->hij", query_block, key_block, preferred_element_type=jnp.float32
        )
        weights = (scores * within).astype(jnp.bfloat16)
        weight_grad = jnp.einsum(
            "ihd,jhd->hij", out_grad_block, value_block, preferred_element_type=jnp.float32
        )
        score_grad = (weight_grad * within).astype(jnp.bfloat16)
        out_grad_wide = out_grad_block.astype(jnp.float32)
        query_parts[block_index] = (
            jnp.einsum("hij,jhd->ihd", score_grad, key_block, preferred_element_type=jnp.float32)
            + jnp.einsum("ihe,hde->ihd", out_grad_wide, state, precision=HIGHEST) * query_decay
        )
        key_parts[block_index] = (
            jnp.einsum("hij,ihd->jhd", score_grad, query_block, preferred_element_type=jnp.float32)
            + jnp.einsum("jhe,hde->jhd", value_block.astype(jnp.float32), carry, precision=HIGHEST)
            * key_decay
        )
        value_parts[block_index] = (
            jnp.einsum("hij,ihd->jhd", weights, out_grad_block, preferred_element_type=jnp.float32)
            + jnp.einsum("jhd,hde->jhe", key_block.astype(jnp.float32), carry, precision=HIGHEST)
            * key_decay
        )
        carry = block_decay * carry + jnp.einsum(
            "ihd,ihe->hde",
            query_block.astype(jnp.float32),
            out_grad_wide * query_decay,
            precision=HIGHEST,
        )
    queries_grad = jnp.concatenate(query_parts, axis=0).reshape(seq_rows, -1)
    keys_grad = jnp.concatenate(key_parts, axis=0).reshape(seq_rows, -1)
    values_grad = jnp.concatenate(value_parts, axis=0).reshape(seq_rows, -1)
    query_pre_grad = (queries_grad * jax.nn.sigmoid(query_pre)).astype(jnp.bfloat16)
    key_pre_grad = (keys_grad * live * jax.nn.sigmoid(key_pre)).astype(jnp.bfloat16)
    value_pre_grad = values_grad.astype(jnp.bfloat16)
    grad_query = inner_rows(hidden_one, query_pre_grad)
    grad_key = inner_rows(hidden_one, key_pre_grad)
    grad_value = inner_rows(hidden_one, value_pre_grad)
    grad_gate_attn = inner_rows(hidden_one, gate_pre_grad)
    partial_one = (
        times_transpose(query_pre_grad, w_query)
        + times_transpose(key_pre_grad, w_key)
        + times_transpose(value_pre_grad, w_value)
        + times_transpose(gate_pre_grad, w_gate_attn)
    )
    hidden_one_grad = lax.psum(partial_one, "tensor")
    grad_gain_one = jnp.sum(hidden_one_grad * normed_one, axis=0)
    input_grad = (
        mid_grad + row_norm_back(hidden_one_grad * gain_one, normed_one, scale_one, 1)
    ).astype(jnp.bfloat16)
    totals = (
        lax.psum_scatter(grad_gain_one, "dp", scatter_dimension=0, tiled=True),
        lax.psum_scatter(grad_query, "dp", scatter_dimension=0, tiled=True),
        lax.psum_scatter(grad_key, "dp", scatter_dimension=0, tiled=True),
        lax.psum_scatter(grad_value, "dp", scatter_dimension=0, tiled=True),
        lax.psum_scatter(grad_gate_attn, "dp", scatter_dimension=0, tiled=True),
        lax.psum_scatter(grad_out, "dp", scatter_dimension=1, tiled=True),
        lax.psum_scatter(grad_gain_two, "dp", scatter_dimension=0, tiled=True),
        lax.psum_scatter(grad_gate, "dp", scatter_dimension=0, tiled=True),
        lax.psum_scatter(grad_up, "dp", scatter_dimension=0, tiled=True),
        lax.psum_scatter(grad_down, "dp", scatter_dimension=1, tiled=True),
    )
    return (
        result,
        input_grad,
        totals[0],
        totals[1],
        totals[2],
        totals[3],
        totals[4],
        totals[5],
        totals[6],
        totals[7],
        totals[8],
        totals[9],
    )


def solution(mesh):
    placed = (
        P("dp", None),
        P("dp"),
        P(),
        P(None, "tensor"),
        P(None, "tensor"),
        P(None, "tensor"),
        P(None, "tensor"),
        P("tensor", None),
        P(),
        P(None, "tensor"),
        P(None, "tensor"),
        P("tensor", None),
        P("dp", None),
    )
    return jax.shard_map(
        shards,
        mesh=mesh,
        in_specs=placed,
        out_specs=(
            P("dp", None),
            P("dp", None),
            P("dp"),
            P("dp", "tensor"),
            P("dp", "tensor"),
            P("dp", "tensor"),
            P("dp", "tensor"),
            P("tensor", "dp"),
            P("dp"),
            P("dp", "tensor"),
            P("dp", "tensor"),
            P("tensor", "dp"),
        ),
        check_vma=False,
    )
```

profile of v0, /device:TPU:0, one launch (start us, length us, event | category | flops | bytes accessed | tf_op | source)
XLA Modules:
  0.0 1129.2 jit_solution(17676534234460012318)
XLA Ops:
  9.7 2.1 fusion.13
  12.6 3.6 fusion.16
  17.1 3.6 fusion.14
  21.8 3.4 convolution_convert_fusion
  25.4 2.4 multiply_convert_fusion.2
  29.3 2.7 multiply_convert_fusion.3
  32.0 1.4 convolution_bitcast_fusion.15
  36.6 3.0 multiply_convert_fusion.11
  40.6 3.3 fusion.83
  44.0 110.7 %all-reduce.8.cloned.1.call-done = f32[1024,1024]{1,0:T(8,128)} async-done(((f32[1024,1024]{1,0:T(8,128)}), f32[1024,1024]{1,0:T(8,128)}) %all-reduce.8.cloned.1.call-update) | async-done | bytes 4194320 | tf_op jit(solution)/shard_map/psum | solution.py:124
  154.7 3.7 multiply_reduce_fusion.2
  158.9 2.9 copy-done.52
  161.8 5.2 fusion.84
  167.0 5.2 fusion.85
  172.2 9.4 multiply_convert_fusion.4
  181.6 3.4 fusion.87
  185.1 5.1 convolution_add_fusion
  190.2 6.8 fusion.86
  197.0 101.2 %all-reduce.10.cloned.1.call-done = f32[1024,1024]{1,0:T(8,128)} async-done(((f32[1024,1024]{1,0:T(8,128)}), f32[1024,1024]{1,0:T(8,128)}) %all-reduce.10.cloned.1.call-update) | async-done | bytes 4194320 | tf_op jit(solution)/shard_map/psum | solution.py:143
  298.2 4.7 multiply_reduce_fusion
  304.1 2.9 convert_add_fusion.1
  307.2 1.6 multiply_reduce_fusion.3
  310.8 2.4 multiply_convert_fusion.1
  314.0 2.4 multiply_convert_fusion
  317.3 1.4 convolution_bitcast_fusion.11
  337.2 3.4 add_add_fusion
  340.6 1.5 copy-done.8
  342.2 4.1 fusion.66
  346.8 4.3 fusion.70
  351.1 4.2 fusion.72
  355.4 5.6 fusion.64
  361.0 4.1 fusion.68
  365.2 8.5 fusion.91
  373.9 8.4 fusion.92
  382.4 8.5 fusion.42
  392.8 146.5 %all-reduce.12.cloned.1.call-done = (f32[1024,1024]{1,0:T(8,128)}, f32[1024,1024]{1,0:T(8,128)}) async-done(((f32[1024,1024]{1,0:T(8,128)}, f32[1024,1024]{1,0:T(8,128)}), (f32[1024,1024]{1,0:T(8,128)}, f32[1024,1024]{1,0:T(8,128)})) %all-reduce.12.cloned.1.call-update) | async-done | bytes 8388624 | tf_op jit(solution)/shard_map/psum | solution.py:133
  539.3 3.3 fusion.12
  542.6 33.9 %all-reduce.2 = (f32[1024]{0:T(1024)S(1)}, f32[1024]{0:T(1024)S(1)}) all-reduce(f32[1024]{0:T(1024)S(1)} %get-tuple-element.14, f32[1024]{0:T(1024)S(1)} %get-tuple-element.12), channel_id=2, replica_groups=mesh['dp'=16,'tensor'=2] {'dp'}, use_global_device_ids=true, to_apply=%region_11.12.clone | all-reduce | flops 2048 | bytes 16384
  577.7 5.4 add_convert_fusion
  585.1 2.3 fusion.11
  587.4 18.0 %reduce-scatter.15.cloned.1.call-done = f32[64,512]{1,0:T(8,128)} async-done(((f32[1024,512]{1,0:T(8,128)}), f32[64,512]{1,0:T(8,128)}) %reduce-scatter.15.cloned.1.call-update) | async-done | bytes 131088 | tf_op jit(solution)/shard_map/reduce_scatter | solution.py:222
  605.4 65.2 %reduce-scatter.11.cloned.1.call-done = f32[64,512]{1,0:T(8,128)} async-done(((f32[1024,512]{1,0:T(8,128)}), f32[64,512]{1,0:T(8,128)}) %reduce-scatter.11.cloned.1.call-update) | async-done | bytes 131088 | tf_op jit(solution)/shard_map/reduce_scatter | solution.py:220
  670.5 64.7 %reduce-scatter.9.cloned.1.call-done = f32[64,512]{1,0:T(8,128)} async-done(((f32[1024,512]{1,0:T(8,128)}), f32[64,512]{1,0:T(8,128)}) %reduce-scatter.9.cloned.1.call-update) | async-done | bytes 131088 | tf_op jit(solution)/shard_map/reduce_scatter | solution.py:219
  735.3 65.3 %reduce-scatter.17.cloned.1.call-done = f32[512,64]{0,1:T(8,128)} async-done(((f32[512,1024]{0,1:T(8,128)}), f32[512,64]{0,1:T(8,128)}) %reduce-scatter.17.cloned.1.call-update) | async-done | bytes 131088 | tf_op jit(solution)/shard_map/reduce_scatter | solution.py:223
  800.6 64.9 %reduce-scatter.13.cloned.1.call-done = f32[64,512]{1,0:T(8,128)} async-done(((f32[1024,512]{1,0:T(8,128)}), f32[64,512]{1,0:T(8,128)}) %reduce-scatter.13.cloned.1.call-update) | async-done | bytes 131088 | tf_op jit(solution)/shard_map/reduce_scatter | solution.py:221
  865.5 85.6 %reduce-scatter.19.cloned.1.call-done = f32[64,1408]{1,0:T(8,128)} async-done(((f32[1024,1408]{1,0:T(8,128)}), f32[64,1408]{1,0:T(8,128)}) %reduce-scatter.19.cloned.1.call-update) | async-done | bytes 360464 | tf_op jit(solution)/shard_map/reduce_scatter | solution.py:225
  951.1 85.6 %reduce-scatter.21.cloned.1.call-done = f32[64,1408]{1,0:T(8,128)} async-done(((f32[1024,1408]{1,0:T(8,128)}), f32[64,1408]{1,0:T(8,128)}) %reduce-scatter.21.cloned.1.call-update) | async-done | bytes 360464 | tf_op jit(solution)/shard_map/reduce_scatter | solution.py:226
  1036.7 85.7 %reduce-scatter.23.cloned.1.call-done = f32[1408,64]{0,1:T(8,128)} async-done(((f32[1408,1024]{0,1:T(8,128)}), f32[1408,64]{0,1:T(8,128)}) %reduce-scatter.23.cloned.1.call-update) | async-done | bytes 360464 | tf_op jit(solution)/shard_map/reduce_scatter | solution.py:227
  (192 shorter events, 39.4 us)
Async XLA Ops:
  7.2 165.0 %copy-start = (bf16[1408,1024]{1,0:T(8,128)(2,1)S(1)}, bf16[1408,1024]{1,0:T(8,128)(2,1)}, u32[]{:S(2)}) copy-start(bf16[1408,1024]{1,0:T(8,128)(2,1)} %param.24) | copy-start | bytes 8650756
  7.2 4.7 copy-start.50
  7.2 147.5 %all-reduce.8.cloned.1.call-start = ((), (), s32[]{:S(2)}) async-start(), calls=%async_computation.8 | async-start | bytes 8388608 | tf_op jit(solution)/shard_map/psum | solution.py:124
  7.2 5.3 copy-start.6
  7.3 5.3 copy-start.54
  12.5 4.5 copy-start.56
  21.8 3.6 copy-start.28
  21.8 3.6 copy-start.30
  21.8 3.6 copy-start.44
  21.8 3.6 copy-start.46
  25.3 2.5 copy-start.24
  25.3 8.1 copy-start.22
  27.7 4.2 copy-start.16
  32.0 2.7 copy-start.18
  34.1 2.5 copy-start.32
  34.7 4.9 copy-start.10
  35.4 4.2 copy-start.12
  36.6 4.0 copy-start.35
  40.6 3.4 copy-start.51
  44.0 254.2 %all-reduce.10.cloned.1.call-start = ((), (), s32[]{:S(2)}) async-start(), calls=%async_computation.9 | async-start | bytes 8388608 | tf_op jit(solution)/shard_map/psum | solution.py:143
  158.4 8.5 copy-start.2
  158.4 3.3 copy-start.52
  161.8 5.2 copy-start.39
  161.8 5.2 copy-start.53
  167.0 5.2 copy-start.42
  181.6 3.4 copy-start.61
  181.6 3.5 copy-start.60
  190.2 349.1 %all-reduce.12.cloned.1.call-start = ((), (), s32[]{:S(2)}) async-start(), calls=%async_computation.18 | async-start | bytes 16777216 | tf_op jit(solution)/shard_map/psum | solution.py:133
  298.2 4.7 copy-start.3
  298.2 5.9 copy-start.20
  304.1 3.0 copy-start.11
  304.1 3.0 copy-start.13
  304.1 3.0 copy-start.14
  304.1 3.1 copy-start.36
  310.8 3.2 copy-start.25
  325.7 11.2 copy-start.34
  340.6 264.8 %reduce-scatter.15.cloned.1.call-start = ((), (), s32[]{:S(2)}) async-start(), calls=%async_computation.13 | async-start | bytes 2228224 | tf_op jit(solution)/shard_map/reduce_scatter | solution.py:222
  346.3 324.2 %reduce-scatter.11.cloned.1.call-start = ((), (), s32[]{:S(2)}) async-start(), calls=%async_computation.11 | async-start | bytes 2228224 | tf_op jit(solution)/shard_map/reduce_scatter | solution.py:220
  351.0 384.2 %reduce-scatter.9.cloned.1.call-start = ((), (), s32[]{:S(2)}) async-start(), calls=%async_computation.10 | async-start | bytes 2228224 | tf_op jit(solution)/shard_map/reduce_scatter | solution.py:219
  355.3 445.3 %reduce-scatter.17.cloned.1.call-start = ((), (), s32[]{:S(2)}) async-start(), calls=%async_computation.14 | async-start | bytes 2228224 | tf_op jit(solution)/shard_map/reduce_scatter | solution.py:223
  361.0 504.6 %reduce-scatter.13.cloned.1.call-start = ((), (), s32[]{:S(2)}) async-start(), calls=%async_computation.12 | async-start | bytes 2228224 | tf_op jit(solution)/shard_map/reduce_scatter | solution.py:221
  365.2 585.9 %reduce-scatter.19.cloned.1.call-start = ((), (), s32[]{:S(2)}) async-start(), calls=%async_computation.15 | async-start | bytes 6127616 | tf_op jit(solution)/shard_map/reduce_scatter | solution.py:225
  373.7 663.0 %reduce-scatter.21.cloned.1.call-start = ((), (), s32[]{:S(2)}) async-start(), calls=%async_computation.16 | async-start | bytes 6127616 | tf_op jit(solution)/shard_map/reduce_scatter | solution.py:226
  382.4 740.1 %reduce-scatter.23.cloned.1.call-start = ((), (), s32[]{:S(2)}) async-start(), calls=%async_computation.17 | async-start | bytes 6127616 | tf_op jit(solution)/shard_map/reduce_scatter | solution.py:227
  577.7 5.4 copy-start.5
  577.7 6.2 copy-start.9
  577.7 7.4 copy-start.15
  577.7 544.7 %copy-start.1 = (bf16[1408,1024]{1,0:T(8,128)(2,1)S(1)}, bf16[1408,1024]{1,0:T(8,128)(2,1)}, u32[]{:S(2)}) copy-start(bf16[1408,1024]{1,0:T(8,128)(2,1)} %param.24) | copy-start | bytes 8650756
  (25 other events, 40.2 us)
Sparse Core Ops, SparseCore 0:
  44.1 110.5 all-reduce.7
  190.3 107.8 all-reduce.9
  340.7 198.5 all-reduce.11
  543.5 61.8 reduce-scatter.14
  610.0 60.5 reduce-scatter.10
  674.7 60.5 reduce-scatter.8
  740.0 60.5 reduce-scatter.16
  804.9 60.5 reduce-scatter.12
  870.5 80.5 reduce-scatter.18
  955.9 80.7 reduce-scatter.20
  1041.7 80.7 reduce-scatter.22
where the time goes:
time: 1140 us; the launch traced here: 1130 us
  waiting for transfers between devices  894 us (78%)
  matrix products  134 us (12%)
  blocking collectives  33.9 us (3%)
  other arithmetic  31.1 us (3%)
  local copies, waits for them, and re-layouts  19.6 us (2%)
  between operations  16.3 us (1%)
    psum x1, waiting for transfers between devices, shards(): ffn_branch = lax.psum(matmul(glu_round, w_down), 'tensor')  147 us
    psum x1, waiting for transfers between devices, shards(): attn_branch = lax.psum(matmul(mixed_round, w_out), 'tensor')  111 us
    psum x1, waiting for transfers between devices, shards(): lax.psum(times_transpose(gate_grad, w_gate) + times_transpose(up_grad, w_...  101 us
    reduce_scatter x1, waiting for transfers between devices, shards(): lax.psum_scatter(grad_down, 'dp', scatter_dimension=1, tiled=True)  85.7 us
    reduce_scatter x1, waiting for transfers between devices, shards(): lax.psum_scatter(grad_up, 'dp', scatter_dimension=0, tiled=True)  85.6 us
    reduce_scatter x1, waiting for transfers between devices, shards(): lax.psum_scatter(grad_gate, 'dp', scatter_dimension=0, tiled=True)  85.6 us
    reduce_scatter x1, waiting for transfers between devices, shards(): lax.psum_scatter(grad_out, 'dp', scatter_dimension=1, tiled=True)  65.3 us
    reduce_scatter x1, waiting for transfers between devices, shards(): lax.psum_scatter(grad_key, 'dp', scatter_dimension=0, tiled=True)  65.2 us
  transfers between devices with their start and end apart: 11, of which 11 were waited for; matrix products, arithmetic and copies ran while one was open for 6% of the time, Pallas kernels for 0%

commit v1 on v0

v1 whole, which is shorter than its diff:
```python
import functools

import jax
import jax.numpy as jnp
from jax import lax
from jax.experimental import pallas as pl
from jax.experimental.pallas import tpu as pltpu
from jax.sharding import PartitionSpec as P

HEADS = 16
HEAD_DIM = 64
BLOCK = 512
EPS = 1e-06
HIGHEST = lax.Precision.HIGHEST
F32 = jnp.float32
BF16 = jnp.bfloat16


def matmul(left, right):
    return jnp.dot(left, right, preferred_element_type=F32)


def times_transpose(left, right):
    return lax.dot_general(left, right, (((1,), (1,)), ((), ())), preferred_element_type=F32)


def row_mean(array):
    return jnp.mean(array, axis=1, keepdims=True)


MIB = 2**20
TILE = 256
CHUNK = 256
PAIR = 2 * HEAD_DIM


def whole(array):
    return pl.BlockSpec(array.shape, lambda *_: (0,) * array.ndim, pipeline_mode=pl.Buffered(1))


def row_tile(columns, rows=TILE):
    return pl.BlockSpec((rows, columns), lambda step: (step, 0))


def call(body, grid, ins, in_specs, outs, out_specs, flops, scratch=(), limit=56):
    return pl.pallas_call(
        body,
        grid=grid,
        in_specs=in_specs,
        out_specs=out_specs,
        out_shape=outs,
        scratch_shapes=scratch,
        cost_estimate=pl.CostEstimate(flops=int(flops), bytes_accessed=8 * MIB, transcendentals=0),
        compiler_params=pltpu.CompilerParams(vmem_limit_bytes=limit * MIB),
    )(*ins)


def shaped(rows, columns, kind=BF16):
    return jax.ShapeDtypeStruct((rows, columns), kind)


def norm_kernel(inputs_ref, gain_ref, hidden_ref):
    wide = inputs_ref[...].astype(F32)
    scale = lax.rsqrt(row_mean(wide * wide) + EPS)
    hidden_ref[...] = (wide * scale * gain_ref[...].astype(F32)).astype(BF16)


def first_norm(inputs, gain):
    rows, width = inputs.shape
    return call(
        norm_kernel,
        (rows // TILE,),
        (inputs, gain),
        [row_tile(width), whole(gain)],
        shaped(rows, width),
        row_tile(width),
        rows * width * 8,
    )


def project_kernel(hidden_ref, live_ref, wq_ref, wk_ref, wv_ref, wg_ref, q_ref, sq_ref, k_ref, sk_ref, v_ref, gate_ref):
    hidden = hidden_ref[...]
    live = live_ref[...]

    def activate(value):
        small = jnp.exp(-jnp.abs(value))
        share = 1.0 / (1.0 + small)
        return jnp.maximum(value, 0.0) + jnp.log1p(small), jnp.where(value >= 0.0, share, small * share)

    positive, slope = activate(matmul(hidden, wq_ref[...]))
    q_ref[...] = positive.astype(BF16)
    sq_ref[...] = slope.astype(BF16)
    positive, slope = activate(matmul(hidden, wk_ref[...]))
    k_ref[...] = (positive * live).astype(BF16)
    sk_ref[...] = (slope * live).astype(BF16)
    v_ref[...] = matmul(hidden, wv_ref[...]).astype(BF16)
    gate_ref[...] = jax.nn.sigmoid(matmul(hidden, wg_ref[...]))


def project(hidden, live, weights):
    rows, width = hidden.shape
    columns = weights[0].shape[1]
    narrow = shaped(rows, columns)
    return call(
        project_kernel,
        (rows // TILE,),
        (hidden, live, *weights),
        [row_tile(width), row_tile(1)] + [whole(w) for w in weights],
        [narrow] * 5 + [shaped(rows, columns, F32)],
        [row_tile(columns)] * 6,
        8 * rows * width * columns,
    )


def head_lanes():
    return lax.broadcasted_iota(jnp.int32, (1, PAIR), 1) < HEAD_DIM


def same_head():
    rows = lax.broadcasted_iota(jnp.int32, (PAIR, PAIR), 0) < HEAD_DIM
    columns = lax.broadcasted_iota(jnp.int32, (PAIR, PAIR), 1) < HEAD_DIM
    return rows == columns


def head_mean(array, ones):
    high = array.astype(BF16)
    low = (array - high.astype(F32)).astype(BF16)
    return (matmul(high, ones) + matmul(low, ones)) * (1.0 / HEAD_DIM)


def decays(rate_ref):
    pair = pl.program_id(0)
    rates = (rate_ref[2 * pair], rate_ref[2 * pair + 1])
    lane_rate = jnp.where(head_lanes(), rates[0], rates[1])
    place = lax.broadcasted_iota(jnp.int32, (CHUNK, 1), 0).astype(F32)
    query_decay = jnp.exp(-lane_rate * (place + 1.0))
    key_decay = jnp.exp(-lane_rate * (CHUNK - 1.0 - place))
    chunk_decay = jnp.exp(-lane_rate * CHUNK)
    return rates, query_decay, key_decay, chunk_decay


def within_table(rate, flipped=False):
    rows = lax.broadcasted_iota(jnp.int32, (CHUNK, CHUNK), 0)
    columns = lax.broadcasted_iota(jnp.int32, (CHUNK, CHUNK), 1)
    spread = columns - rows if flipped else rows - columns
    kept = spread >= 0
    return jnp.where(kept, jnp.exp(-rate * jnp.where(kept, spread, 0).astype(F32)), 0.0)


def attend_kernel(rate_ref, q_ref, k_ref, v_ref, gate_ref, attended_ref, mixed_ref):
    rates, query_decay, key_decay, chunk_decay = decays(rate_ref)
    first = head_lanes()
    same = same_head()
    ones = jnp.where(same, 1.0, 0.0).astype(BF16)
    tables = [within_table(rate) for rate in rates]
    masks = [jnp.where(first, 1.0, 0.0).astype(BF16), jnp.where(first, 0.0, 1.0).astype(BF16)]
    state = jnp.zeros((PAIR, PAIR), F32)
    for index in range(q_ref.shape[0] // CHUNK):
        rows = pl.ds(index * CHUNK, CHUNK)
        q, k, v = q_ref[rows, :], k_ref[rows, :], v_ref[rows, :]
        attended = matmul(q, state.astype(BF16)) * query_decay
        for mask, table in zip(masks, tables):
            weights = (times_transpose(q * mask, k) * table).astype(BF16)
            attended = attended + matmul(weights, v * mask)
        keys = (k.astype(F32) * key_decay).T.astype(BF16)
        state = chunk_decay * state + jnp.where(same, matmul(keys, v), 0.0)
        scale = lax.rsqrt(head_mean(attended * attended, ones) + EPS)
        attended_ref[rows, :] = attended
        mixed_ref[rows, :] = (attended * scale * gate_ref[rows, :]).astype(BF16)


def pair_spec(rows):
    return pl.BlockSpec((rows, PAIR), lambda pair: (0, pair))


def attend(q, k, v, gate, rates):
    rows, columns = q.shape
    return call(
        attend_kernel,
        (columns // PAIR,),
        (rates, q, k, v, gate),
        [pl.BlockSpec(memory_space=pltpu.SMEM)] + [pair_spec(rows)] * 4,
        [shaped(rows, columns, F32), shaped(rows, columns)],
        [pair_spec(rows)] * 2,
        12 * rows * columns * CHUNK,
    )


def attend_back_kernel(
    rate_ref, q_ref, sq_ref, k_ref, sk_ref, v_ref, gate_ref, attended_ref, grad_ref, wo_ref,
    dq_ref, dk_ref, dv_ref, dg_ref, out_grad, states,
):
    rates, query_decay, key_decay, chunk_decay = decays(rate_ref)
    first = head_lanes()
    same = same_head()
    ones = jnp.where(same, 1.0, 0.0).astype(BF16)
    tables = [within_table(rate) for rate in rates]
    flipped = [within_table(rate, True) for rate in rates]
    masks = [jnp.where(first, 1.0, 0.0).astype(BF16), jnp.where(first, 0.0, 1.0).astype(BF16)]
    chunks = q_ref.shape[0] // CHUNK
    state = jnp.zeros((PAIR, PAIR), F32)
    for index in range(chunks):
        rows = pl.ds(index * CHUNK, CHUNK)
        mixed_grad = times_transpose(grad_ref[rows, :], wo_ref[...])
        attended, gate = attended_ref[rows, :], gate_ref[rows, :]
        scale = lax.rsqrt(head_mean(attended * attended, ones) + EPS)
        normed = attended * scale
        dg_ref[rows, :] = (mixed_grad * normed * gate * (1.0 - gate)).astype(BF16)
        normed_grad = mixed_grad * gate
        out_grad[rows, :] = (scale * (normed_grad - normed * head_mean(normed_grad * normed, ones))).astype(BF16)
        states[index] = state.astype(BF16)
        if index < chunks - 1:
            keys = (k_ref[rows, :].astype(F32) * key_decay).T.astype(BF16)
            state = chunk_decay * state + jnp.where(same, matmul(keys, v_ref[rows, :]), 0.0)
    carry = jnp.zeros((PAIR, PAIR), F32)
    for index in reversed(range(chunks)):
        rows = pl.ds(index * CHUNK, CHUNK)
        q, k, v, grad = q_ref[rows, :], k_ref[rows, :], v_ref[rows, :], out_grad[rows, :]
        narrow = carry.astype(BF16)
        dq = times_transpose(grad, states[index]) * query_decay
        dk = times_transpose(v, narrow) * key_decay
        dv = matmul(k, narrow) * key_decay
        for mask, table, turned in zip(masks, tables, flipped):
            q_one, grad_one = q * mask, grad * mask
            weights = (times_transpose(k, q_one) * turned).astype(BF16)
            dv = dv + matmul(weights, grad_one)
            dq = dq + matmul((times_transpose(grad_one, v) * table).astype(BF16), k * mask)
            dk = dk + matmul((times_transpose(v, grad_one) * turned).astype(BF16), q_one)
        dq_ref[rows, :] = (dq * sq_ref[rows, :].astype(F32)).astype(BF16)
        dk_ref[rows, :] = (dk * sk_ref[rows, :].astype(F32)).astype(BF16)
        dv_ref[rows, :] = dv.astype(BF16)
        if index > 0:
            turned_q = q.astype(F32).T.astype(BF16)
            decayed = (grad.astype(F32) * query_decay).astype(BF16)
            carry = chunk_decay * carry + jnp.where(same, matmul(turned_q, decayed), 0.0)


def attend_back(half, out_grad, w_out):
    q, sq, k, sk, v, gate, attended, rates = half
    rows, columns = q.shape
    width = out_grad.shape[1]
    return call(
        attend_back_kernel,
        (columns // PAIR,),
        (rates, q, sq, k, sk, v, gate, attended, out_grad, w_out),
        [pl.BlockSpec(memory_space=pltpu.SMEM)]
        + [pair_spec(rows)] * 7
        + [whole(out_grad), pl.BlockSpec((PAIR, width), lambda pair: (pair, 0))],
        [shaped(rows, columns)] * 4,
        [pair_spec(rows)] * 4,
        2 * rows * columns * width + 30 * rows * columns * CHUNK,
        scratch=[pltpu.VMEM((rows, PAIR), BF16), pltpu.VMEM((rows // CHUNK, PAIR, PAIR), BF16)],
    )


def glu_parts(hidden, out_grad, wg_ref, wu_ref, wd_ref, columns):
    gate_pre = matmul(hidden, wg_ref[:, columns])
    up_pre = matmul(hidden, wu_ref[:, columns])
    glu_grad = times_transpose(out_grad, wd_ref[columns, :])
    logistic = jax.nn.sigmoid(gate_pre)
    act = gate_pre * logistic
    glu = (act * up_pre).astype(BF16)
    up_grad = (glu_grad * act).astype(BF16)
    gate_grad = (glu_grad * up_pre * (logistic * (1.0 + gate_pre * (1.0 - logistic)))).astype(BF16)
    return glu, gate_grad, up_grad


def unit_slices(units):
    step = 512
    return [slice(low, min(low + step, units)) for low in range(0, units, step)]


def middle_kernel(
    inputs_ref, live_ref, dy_ref, mixed_a_ref, mixed_b_ref, wo_a_ref, wo_b_ref, gain_ref, wg_ref, wu_ref, wd_ref,
    residual_ref, hidden_ref, glu_ref, gate_grad_ref, up_grad_ref, branch_ref, back_ref,
):
    live = live_ref[...]
    branch = matmul(mixed_a_ref[...], wo_a_ref[...]) + matmul(mixed_b_ref[...], wo_b_ref[...])
    residual = inputs_ref[...].astype(F32) + live * branch
    residual_ref[...] = residual
    scale = lax.rsqrt(row_mean(residual * residual) + EPS)
    hidden = (residual * scale * gain_ref[...].astype(F32)).astype(BF16)
    hidden_ref[...] = hidden
    out_grad = (live * dy_ref[...].astype(F32)).astype(BF16)
    units = wg_ref.shape[1]
    for columns in unit_slices(units):
        glu, gate_grad, up_grad = glu_parts(hidden, out_grad, wg_ref, wu_ref, wd_ref, columns)
        glu_ref[:, columns] = glu
        gate_grad_ref[:, columns] = gate_grad
        up_grad_ref[:, columns] = up_grad
    branch_ref[...] = matmul(glu_ref[...], wd_ref[...])
    back_ref[...] = times_transpose(gate_grad_ref[...], wg_ref[...]) + times_transpose(up_grad_ref[...], wu_ref[...])


def middle(inputs, live, dy, mixed, outs, gain, glus):
    rows, width = inputs.shape
    heads = mixed[0].shape[1]
    units = glus[0].shape[1]
    return call(
        middle_kernel,
        (rows // TILE,),
        (inputs, live, dy, *mixed, *outs, gain, *glus),
        [row_tile(width), row_tile(1), row_tile(width), row_tile(heads), row_tile(heads)]
        + [whole(w) for w in (*outs, gain, *glus)],
        [shaped(rows, width, F32), shaped(rows, width)]
        + [shaped(rows, units)] * 3
        + [shaped(rows, width, F32)] * 2,
        [row_tile(width)] * 2 + [row_tile(units)] * 3 + [row_tile(width)] * 2,
        2 * rows * width * (2 * heads + 6 * units),
    )


def norm_back(grad, normed, scale):
    return scale * (grad - normed * row_mean(grad * normed))


def middle_back_kernel(
    residual_ref, hidden_ref, live_ref, dy_ref, branch_ref, back_ref, gain_ref, wg_ref, wu_ref, wd_ref,
    result_ref, mid_ref, grad_ref, gain_grad_ref, glu_buf, gate_buf, up_buf,
):
    live = live_ref[...]
    dy = dy_ref[...].astype(F32)
    hidden = hidden_ref[...]
    out_grad = (live * dy).astype(BF16)
    for columns in unit_slices(wg_ref.shape[1]):
        glu_buf[:, columns], gate_buf[:, columns], up_buf[:, columns] = glu_parts(
            hidden, out_grad, wg_ref, wu_ref, wd_ref, columns
        )
    residual = residual_ref[...]
    branch = branch_ref[...] + matmul(glu_buf[...], wd_ref[...])
    result_ref[...] = (residual + live * branch).astype(BF16)
    back = back_ref[...] + times_transpose(gate_buf[...], wg_ref[...]) + times_transpose(up_buf[...], wu_ref[...])
    scale = lax.rsqrt(row_mean(residual * residual) + EPS)
    normed = residual * scale

    @pl.when(pl.program_id(0) == 0)
    def _():
        gain_grad_ref[...] = jnp.zeros_like(gain_grad_ref)

    gain_grad_ref[...] += jnp.sum(back * normed, axis=0, keepdims=True)
    mid = dy + norm_back(back * gain_ref[...].astype(F32), normed, scale)
    mid_ref[...] = mid
    grad_ref[...] = (live * mid).astype(BF16)


def middle_back(residual, hidden, live, dy, branch, back, gain, glus):
    rows, width = hidden.shape
    units = glus[0].shape[1]
    return call(
        middle_back_kernel,
        (rows // TILE,),
        (residual, hidden, live, dy, branch, back, gain, *glus),
        [row_tile(width), row_tile(width), row_tile(1)]
        + [row_tile(width)] * 3
        + [whole(w) for w in (gain, *glus)],
        [shaped(rows, width), shaped(rows, width, F32), shaped(rows, width), shaped(1, width, F32)],
        [row_tile(width)] * 3 + [pl.BlockSpec((1, width), lambda step: (0, 0))],
        2 * rows * width * 6 * units,
        scratch=[pltpu.VMEM((TILE, units), BF16)] * 3,
    )


def first_back_kernel(inputs_ref, mid_ref, gain_ref, *refs):
    grads, weights, (result_ref, gain_grad_ref) = refs[:8], refs[8:16], refs[16:]
    back = times_transpose(grads[0][...], weights[0][...])
    for grad, weight in zip(grads[1:], weights[1:]):
        back = back + times_transpose(grad[...], weight[...])
    wide = inputs_ref[...].astype(F32)
    scale = lax.rsqrt(row_mean(wide * wide) + EPS)
    normed = wide * scale

    @pl.when(pl.program_id(0) == 0)
    def _():
        gain_grad_ref[...] = jnp.zeros_like(gain_grad_ref)

    gain_grad_ref[...] += jnp.sum(back * normed, axis=0, keepdims=True)
    result_ref[...] = (mid_ref[...] + norm_back(back * gain_ref[...].astype(F32), normed, scale)).astype(BF16)


def first_back(inputs, mid, gain, grads, weights):
    rows, width = inputs.shape
    columns = weights[0].shape[1]
    return call(
        first_back_kernel,
        (rows // TILE,),
        (inputs, mid, gain, *grads, *weights),
        [row_tile(width), row_tile(width), whole(gain)]
        + [row_tile(columns)] * 8
        + [whole(w) for w in weights],
        [shaped(rows, width), shaped(1, width, F32)],
        [row_tile(width), pl.BlockSpec((1, width), lambda step: (0, 0))],
        2 * rows * width * columns * 8,
    )


def product_kernel(left_ref, right_ref, *refs):
    total = matmul(left_ref[...], right_ref[...])
    if len(refs) == 2:
        total = total + refs[0][...]
    refs[-1][...] = total


def product(left, right, first, count, came=None, came_first=0):
    depth, columns = right.shape
    tile = min(TILE, count)
    ins = [left, right]
    specs = [pl.BlockSpec((tile, depth), lambda step: (first // tile + step, 0)), whole(right)]
    if came is not None:
        ins.append(came)
        specs.append(pl.BlockSpec((tile, columns), lambda step: (came_first // tile + step, 0)))
    return call(
        product_kernel,
        (count // tile,),
        tuple(ins),
        specs,
        shaped(count, columns, F32),
        row_tile(columns, tile),
        2 * count * depth * columns,
    )


CORE, ACROSS_X, NEAR_Z, FAR_Z = 1, 2, 4, 8


def swap_dp(array, bit, size):
    return lax.ppermute(array, "dp", [(place, place ^ bit) for place in range(size)])


def swap_tensor(array):
    return lax.ppermute(array, "tensor", [(0, 1), (1, 0)])


def place_kernel(place_ref, *refs):
    step = pl.program_id(0)
    for index in range(8):

        @pl.when(step == index)
        def _(index=index):
            refs[8][...] = refs[index][...].astype(BF16)


def cast_kernel(wide_ref, out_ref):
    out_ref[...] = wide_ref[...].astype(BF16)


def cast_weight(wide):
    rows, columns = wide.shape
    spec = pl.BlockSpec((rows // 8, columns), lambda row: (row, 0))
    return pl.pallas_call(
        cast_kernel, grid=(8,), out_shape=jax.ShapeDtypeStruct(wide.shape, BF16), in_specs=[spec], out_specs=spec
    )(wide)


def gather_other(weights, place, dp_size):
    if dp_size != 16:
        return [cast_weight(swap_tensor(weight.astype(F32))) for weight in weights]
    count = len(weights)
    rows, columns = weights[0].shape
    part = rows // 8

    def piece(index):
        return jnp.concatenate(
            [lax.dynamic_slice_in_dim(w, index * part, part, 0).astype(F32) for w in weights], axis=0
        )

    own = swap_tensor(piece(place))
    diagonal = swap_tensor(piece(place ^ 6))
    from_x = swap_dp(own, ACROSS_X, 16)
    from_z = swap_dp(own, NEAR_Z, 16)
    even = {0: own, 2: from_x, 4: from_z, 6: diagonal}
    odd = {index + 1: swap_dp(array, CORE, 16) for index, array in even.items()}
    pieces = {**even, **odd}
    placed = []
    for which in range(count):
        placed.append(
            pl.pallas_call(
                place_kernel,
                out_shape=jax.ShapeDtypeStruct((rows, columns), BF16),
                grid_spec=pltpu.PrefetchScalarGridSpec(
                    num_scalar_prefetch=1,
                    grid=(8,),
                    in_specs=[pl.BlockSpec((part, columns), lambda step, ref, which=which: (which, 0))] * 8,
                    out_specs=pl.BlockSpec((part, columns), lambda step, ref: (ref[0] ^ step, 0)),
                ),
                compiler_params=pltpu.CompilerParams(vmem_limit_bytes=40 * 2**20),
            )(place.reshape(1), *[pieces[index] for index in range(8)])
        )
    return placed


def relative_rows(array, dp_place, order, dp_size):
    if dp_size != 16:
        return array
    blocks = array.reshape(2, 2, 2, 2, array.shape[0] // 16, array.shape[1])
    for axis, bit in enumerate((FAR_Z, NEAR_Z, ACROSS_X, CORE)):
        blocks = jnp.where((dp_place & bit) > 0, jnp.flip(blocks, axis), blocks)
    axes = {FAR_Z: 0, NEAR_Z: 1, ACROSS_X: 2, CORE: 3}
    return blocks.transpose([axes[bit] for bit in order] + [4, 5]).reshape(array.shape)


def scatter_product(left, right, order, dp_size):
    if dp_size != 16:
        return lax.psum_scatter(matmul(left, right), "dp", scatter_dimension=0, tiled=True)
    size = left.shape[0]
    half = size // 4
    came = swap_dp(product(left, right, 2 * half, 2 * half), order[0], 16)
    came_next = swap_dp(product(left, right, half, half, came, half), order[1], 16)
    kept = product(left, right, 0, half, came, 0)
    for bit in order[2:]:
        half = kept.shape[0] // 2
        send = kept[half:] + came_next[half:]
        kept = kept[:half] + came_next[:half]
        came_next = swap_dp(send, bit, 16)
    return kept + came_next


def scatter_vector(vector, dp_place, dp_size):
    if dp_size != 16:
        return lax.psum_scatter(vector, "dp", scatter_dimension=0, tiled=True)
    order = (CORE, ACROSS_X, NEAR_Z, FAR_Z)
    kept = relative_rows(vector, dp_place, order, dp_size)
    for bit in order:
        half = kept.shape[0] // 2
        kept = kept[:half] + swap_dp(kept[half:], bit, 16)
    return kept


def shards_here(
    dp_size, inputs, lengths, gain_attn, w_query, w_key, w_value, w_gate_attn, w_out, gain_ffn, w_gate, w_up, w_down, cotangent
):
    seq_rows = inputs.shape[0]
    local_heads = w_query.shape[1] // HEAD_DIM
    side = lax.axis_index("tensor")
    dp_place = lax.axis_index("dp")
    place = dp_place % 8
    others_qk = gather_other([w_query, w_key], place, dp_size)
    others_vg = gather_other([w_value, w_gate_attn], place, dp_size)
    others_out = gather_other([w_out], place, dp_size)
    others_gu = gather_other([w_gate, w_up], place, dp_size)
    others_down = gather_other([w_down], place, dp_size)
    projections = ((w_query, w_key, w_value, w_gate_attn), tuple(others_qk) + tuple(others_vg))
    outs = (w_out, others_out[0])
    glus = ((w_gate, w_up, w_down), (others_gu[0], others_gu[1], others_down[0]))
    head_ids = jnp.arange(local_heads)
    rates = tuple(
        jnp.exp2(-8.0 * ((which * local_heads + head_ids).astype(F32) + 1.0) / HEADS)
        for which in (side, 1 - side)
    )
    positions = jnp.arange(seq_rows, dtype=jnp.int32)
    live = (positions < lengths[0]).astype(F32)[:, None]
    gain_one = gain_attn.reshape(1, -1)
    gain_two = gain_ffn.reshape(1, -1)
    ffn_out_grad = (live * cotangent.astype(F32)).astype(BF16)

    hidden_one = first_norm(inputs, gain_one)
    halves = []
    mixed = []
    for half in range(2):
        parts = project(hidden_one, live, projections[half])
        q, sq, k, sk, v, gate = parts
        attended, mixed_half = attend(q, k, v, gate, rates[half])
        halves.append((*parts, attended, rates[half]))
        mixed.append(mixed_half)
    residual, hidden_two, glu, gate_grad, up_grad, branch, back = middle(
        inputs, live, cotangent, mixed, outs, gain_two, glus[0]
    )
    order = (CORE, ACROSS_X, NEAR_Z, FAR_Z)
    order_z = (CORE, NEAR_Z, FAR_Z, ACROSS_X)
    ffn_out_grad_t = relative_rows(ffn_out_grad.T, dp_place, order_z, dp_size)
    grad_down = scatter_product(ffn_out_grad_t, glu, order_z, dp_size)
    hidden_two_t = relative_rows(hidden_two.T, dp_place, order, dp_size)
    grad_gate = scatter_product(hidden_two_t, gate_grad, order, dp_size)
    grad_up = scatter_product(hidden_two_t, up_grad, order, dp_size)
    result, mid_grad, attn_out_grad, gain_two_grad = middle_back(
        residual, hidden_two, live, cotangent, branch, back, gain_two, glus[1]
    )
    attn_out_grad_t = relative_rows(attn_out_grad.T, dp_place, order, dp_size)
    hidden_one_t = relative_rows(hidden_one.T, dp_place, order, dp_size)
    own = attend_back(halves[0], attn_out_grad, outs[0])
    grad_out = scatter_product(attn_out_grad_t, mixed[0], order, dp_size)
    grad_query, grad_key, grad_value, grad_gate_attn = [
        scatter_product(hidden_one_t, grad, order, dp_size) for grad in own
    ]
    other = attend_back(halves[1], attn_out_grad, outs[1])
    input_grad, gain_one_grad = first_back(
        inputs, mid_grad, gain_one, (*own, *other), (*projections[0], *projections[1])
    )
    gains = scatter_vector(
        jnp.concatenate([gain_one_grad, gain_two_grad], axis=0).T, dp_place, dp_size
    )
    return (
        result,
        input_grad,
        gains[:, 0],
        grad_query,
        grad_key,
        grad_value,
        grad_gate_attn,
        grad_out.T,
        gains[:, 1],
        grad_gate,
        grad_up,
        grad_down.T,
    )


def solution(mesh):
    placed = (
        P("dp", None),
        P("dp"),
        P(),
        P(None, "tensor"),
        P(None, "tensor"),
        P(None, "tensor"),
        P(None, "tensor"),
        P("tensor", None),
        P(),
        P(None, "tensor"),
        P(None, "tensor"),
        P("tensor", None),
        P("dp", None),
    )
    return jax.shard_map(
        functools.partial(shards_here, mesh.shape["dp"]),
        mesh=mesh,
        in_specs=placed,
        out_specs=(
            P("dp", None),
            P("dp", None),
            P("dp"),
            P("dp", "tensor"),
            P("dp", "tensor"),
            P("dp", "tensor"),
            P("dp", "tensor"),
            P("tensor", "dp"),
            P("dp"),
            P("dp", "tensor"),
            P("dp", "tensor"),
            P("tensor", "dp"),
        ),
        check_vma=False,
    )
```

time: 1140 us -> 619 us (0.54)
  waiting for transfers between devices: 894 us -> 196 us
  Pallas kernels: 0 us -> 265 us
  matrix products: 134 us -> 0 us
  starting transfers between devices: 1.03 us -> 51.3 us
  blocking collectives: 33.9 us -> 0 us
  local copies, waits for them, and re-layouts: 19.6 us -> 42.6 us
  other arithmetic: 31.1 us -> 51.7 us
  between operations: 16.3 us -> 2.5 us
    reduce_scatter x8 -> x0, waiting for transfers between devices: 535 us -> none  [the longest x1 85.7 us: shards(): lax.psum_scatter(grad_down, 'dp', scatter_dimension=1, tiled=True)]
    psum x3 -> x0, waiting for transfers between devices: 358 us -> none  [the longest x1 147 us: shards(): ffn_branch = lax.psum(matmul(glu_round, w_down), 'tensor')]
    pallas_call x0 -> x42, Pallas kernels: none -> 265 us  [the longest x34 248 us: call(): pl.pallas_call(body, grid=grid, in_specs=in_specs, out_specs=out_specs, o...]
    ppermute x0 -> x76, waiting for transfers between devices: none -> 196 us  [the longest x66 163 us: swap_dp(): lax.ppermute(array, 'dp', [(place, place ^ bit) for place in range(size)])]
    dot_general x46 -> x0, matrix products: 134 us -> none  [the longest x8 47.6 us: inner_rows(): lax.dot_general(left, right, (((0,), (0,)), ((), ())), preferred_element_...]
    ppermute x0 -> x76, starting transfers between devices: none -> 51.3 us  [the longest x66 38.5 us: swap_dp(): lax.ppermute(array, 'dp', [(place, place ^ bit) for place in range(size)])]
    unnamed x1 -> x0, blocking collectives: 33.9 us -> none
    select_n x0 -> x14, other arithmetic: none -> 19 us  [relative_rows(): blocks = jnp.where(dp_place & bit > 0, jnp.flip(blocks, axis), blocks)]
  transfers between devices with their start and end apart: 11 -> 76, of which waited for: 11 -> 28; matrix products, arithmetic and copies ran while one was open for 6% -> 12% of each run, Pallas kernels for 0% -> 44%
where the time goes in v1:
time: 619 us; the launch traced here: 609 us
  Pallas kernels  265 us (43%)
  waiting for transfers between devices  196 us (32%)
  other arithmetic  51.7 us (8%)
  starting transfers between devices  51.3 us (8%)
  local copies, waits for them, and re-layouts  42.6 us (7%)
    pallas_call x34, Pallas kernels, call(): pl.pallas_call(body, grid=grid, in_specs=in_specs, out_specs=out_specs, o...  248 us
    ppermute x66, waiting for transfers between devices, swap_dp(): lax.ppermute(array, 'dp', [(place, place ^ bit) for place in range(size)])  163 us
    ppermute x66, starting transfers between devices, swap_dp(): lax.ppermute(array, 'dp', [(place, place ^ bit) for place in range(size)])  38.5 us
    ppermute x10, waiting for transfers between devices, swap_tensor(): return lax.ppermute(array, 'tensor', [(0, 1), (1, 0)])  33.1 us
    unnamed x119, local copies, waits for them, and re-layouts  19.5 us
    select_n x14, other arithmetic, relative_rows(): blocks = jnp.where(dp_place & bit > 0, jnp.flip(blocks, axis), blocks)  19 us
    pallas_call x8, Pallas kernels, gather_other(): pl.pallas_call(place_kernel, out_shape=jax.ShapeDtypeStruct((rows, column...  16.5 us
    ppermute x10, starting transfers between devices, swap_tensor(): return lax.ppermute(array, 'tensor', [(0, 1), (1, 0)])  12.8 us
  transfers between devices with their start and end apart: 76, of which 28 were waited for; matrix products, arithmetic and copies ran while one was open for 12% of the time, Pallas kernels for 44%

profile of v1, /device:TPU:0, one launch (start us, length us, event | category | flops | bytes accessed | tf_op | source)
XLA Modules:
  0.0 608.9 jit_solution(11132781990181312685)
XLA Ops:
  17.4 4.1 shard_map.220.hidden_ref
  21.5 3.9 copy.40
  32.5 10.4 %shard_map.221 = (bf16[1024,512]{1,0:T(8,128)(2,1)}, bf16[1024,512]{1,0:T(8,128)(2,1)}, bf16[1024,512]{1,0:T(8,128)(2,1)}, bf16[1024,512]{1,0:T(8,128)(2,1)}, bf...) custom-call(bf16[1024,1024]{1,0:T(8,128)(2,1)} %shard_map.220.hidden_ref, f32[1024,1]{1,0:T(8,128)} %fusion.4.live_ref, ...), custom_call_target="tpu_custom_call" | custom-call | flops 4294967296 | bytes 8388608 | tf_op jit(solution)/shard_map/pallas_call | solution.py:46
  42.9 14.2 %collective-permute-done.16.refs_0_ = f32[64,1024]{1,0:T(8,128)S(1)} collective-permute-done((f32[64,1024]{1,0:T(8,128)}, f32[64,1024]{1,0:T(8,128)S(1)}, u32[]{:S(2)}, u32[]{:S(2)}) %collective-permute-start.16) | collective-permute-done | bytes 262176 | tf_op jit(solution)/shard_map/ppermute | solution.py:430
  71.6 4.5 reverse_select_fusion.1
  84.5 6.5 %collective-permute-done.10.refs_2_ = f32[256,512]{1,0:T(8,128)} collective-permute-done((f32[256,512]{1,0:T(8,128)S(1)}, f32[256,512]{1,0:T(8,128)}, u32[]{:S(2)}, u32[]{:S(2)}) %collective-permute-start.10) | collective-permute-done | bytes 524320 | tf_op jit(solution)/shard_map/ppermute | solution.py:426
  95.2 6.1 %collective-permute-done.2.refs_2_ = f32[256,512]{1,0:T(8,128)} collective-permute-done((f32[256,512]{1,0:T(8,128)}, f32[256,512]{1,0:T(8,128)}, u32[]{:S(2)}, u32[]{:S(2)}) %collective-permute-start.2) | collective-permute-done | bytes 524320 | tf_op jit(solution)/shard_map/ppermute | solution.py:426
  104.5 4.6 fusion.3
  109.7 3.4 fusion
  119.4 8.7 %shard_map.222 = (f32[1024,512]{1,0:T(8,128)}, bf16[1024,512]{1,0:T(8,128)(2,1)}) custom-call(f32[8]{0:T(128)} %multiply_exponential_fusion.1.rate_ref, bf16[1024,512]{1,0:T(8,128)(2,1)} %get-tuple-element.49.q_ref, bf16[1024,512]{1,0:T(8,128)(2,1)} %get-tuple-element.50.k_ref, bf16[1024,512]{1,0:T(8,128)(2,1)} %get-tuple-element.51.v_ref, ...), custom_call_target="tpu_custom_call" | custom-call | flops 1610612736 | bytes 8388608 | tf_op jit(solution)/shard_map/pallas_call | solution.py:46
  145.3 10.4 %shard_map.227 = (bf16[1024,512]{1,0:T(8,128)(2,1)}, bf16[1024,512]{1,0:T(8,128)(2,1)}, bf16[1024,512]{1,0:T(8,128)(2,1)}, bf16[1024,512]{1,0:T(8,128)(2,1)}, bf...) custom-call(bf16[1024,1024]{1,0:T(8,128)(2,1)} %shard_map.220.hidden_ref, f32[1024,1]{1,0:T(8,128)} %fusion.4.live_ref, ...), custom_call_target="tpu_custom_call" | custom-call | flops 4294967296 | bytes 8388608 | tf_op jit(solution)/shard_map/pallas_call | solution.py:46
  155.7 8.3 %shard_map.228 = (f32[1024,512]{1,0:T(8,128)}, bf16[1024,512]{1,0:T(8,128)(2,1)}) custom-call(f32[8]{0:T(128)} %multiply_exponential_fusion.rate_ref, bf16[1024,512]{1,0:T(8,128)(2,1)} %get-tuple-element.54.q_ref, bf16[1024,512]{1,0:T(8,128)(2,1)} %get-tuple-element.55.k_ref, bf16[1024,512]{1,0:T(8,128)(2,1)} %get-tuple-element.56.v_ref, ...), custom_call_target="tpu_custom_call" | custom-call | flops 1610612736 | bytes 8388608 | tf_op jit(solution)/shard_map/pallas_call | solution.py:46
  164.0 16.7 %collective-permute-done.38.refs_6_ = f32[176,1024]{1,0:T(8,128)} collective-permute-done((f32[176,1024]{1,0:T(8,128)}, f32[176,1024]{1,0:T(8,128)}, u32[]{:S(2)}, u32[]{:S(2)}) %collective-permute-start.38) | collective-permute-done | bytes 720928 | tf_op jit(solution)/shard_map/ppermute | solution.py:430
  181.9 31.0 %shard_map.230 = (f32[1024,1024]{1,0:T(8,128)}, bf16[1024,1024]{1,0:T(8,128)(2,1)}, bf16[1024,1408]{1,0:T(8,128)(2,1)}, bf16[1024,1408]{1,0:T(8,128)(2,1)}, bf16...) custom-call(bf16[1024,1024]{1,0:T(8,128)(2,1)} %inputs_ref.5, f32[1024,1]{1,0:T(8,128)} %fusion.4.live_ref, ...), custom_call_target="tpu_custom_call" | custom-call | flops 19864223744 | bytes 8388608 | tf_op jit(solution)/shard_map/pallas_call | solution.py:46
  212.9 4.3 copy.44
  218.4 3.2 reverse_select_fusion.7
  226.1 5.2 shard_map.256
  231.3 5.1 shard_map.253
  236.3 5.1 shard_map.259
  242.8 3.2 shard_map.233.wd_ref
  250.4 3.3 shard_map.232.wu_ref
  255.3 29.4 %shard_map.234 = (bf16[1024,1024]{1,0:T(8,128)(2,1)}, f32[1024,1024]{1,0:T(8,128)}, bf16[1024,1024]{1,0:T(8,128)(2,1)}, f32[1,1024]{1,0:T(1,128)}) custom-call(f32[1024,1024]{1,0:T(8,128)} %get-tuple-element.59.residual_ref, bf16[1024,1024]{1,0:T(8,128)(2,1)} %get-tuple-element.60.hidden_ref, f32[1024,1]{1,0:T(8,128)} %fusion.4.live_ref, ...), custom_call_target="tpu_custom_call" | custom-call | flops 17716740096 | bytes 8388608 | tf_op jit(solution)/shard_map/pallas_call | solution.py:46
  284.6 21.6 %shard_map.235 = (bf16[1024,512]{1,0:T(8,128)(2,1)}, bf16[1024,512]{1,0:T(8,128)(2,1)}, bf16[1024,512]{1,0:T(8,128)(2,1)}, bf16[1024,512]{1,0:T(8,128)(2,1)}) custom-call(f32[8]{0:T(128)} %multiply_exponential_fusion.1.rate_ref, bf16[1024,512]{1,0:T(8,128)(2,1)} %get-tuple-element.49.q_ref, bf16[1024,512]{1,0:T(8,128)(2,1)} %get-tuple-element.65.sq_ref, ...), custom_call_target="tpu_custom_call" | custom-call | flops 5100273664 | bytes 8388608 | tf_op jit(solution)/shard_map/pallas_call | solution.py:46
  306.2 21.4 %shard_map.236 = (bf16[1024,512]{1,0:T(8,128)(2,1)}, bf16[1024,512]{1,0:T(8,128)(2,1)}, bf16[1024,512]{1,0:T(8,128)(2,1)}, bf16[1024,512]{1,0:T(8,128)(2,1)}) custom-call(f32[8]{0:T(128)} %multiply_exponential_fusion.rate_ref, bf16[1024,512]{1,0:T(8,128)(2,1)} %get-tuple-element.54.q_ref, bf16[1024,512]{1,0:T(8,128)(2,1)} %get-tuple-element.73.sq_ref, ...), custom_call_target="tpu_custom_call" | custom-call | flops 5100273664 | bytes 8388608 | tf_op jit(solution)/shard_map/pallas_call | solution.py:46
  327.6 17.3 %shard_map.237 = (bf16[1024,1024]{1,0:T(8,128)(2,1)}, f32[1,1024]{1,0:T(1,128)}) custom-call(bf16[1024,1024]{1,0:T(8,128)(2,1)} %inputs_ref.5, f32[1024,1024]{1,0:T(8,128)} %get-tuple-element.64.mid_ref, bf16[1,1024]{1,0:T(2,128)(2,1)} %reshape.81.gain_ref, bf16[1024,512]{1,0:T(8,128)(2,1)} %get-tuple-element.69.refs_0_.right_ref, ...), custom_call_target="tpu_custom_call" | custom-call | flops 8589934592 | bytes 8388608 | tf_op jit(solution)/shard_map/pallas_call | solution.py:46
  360.0 3.1 shard_map.247
  366.0 4.5 shard_map.261
  374.0 3.1 shard_map.241
  380.7 4.9 shard_map.258
  386.7 4.5 shard_map.260
  391.1 4.5 shard_map.255
  397.3 4.5 shard_map.257
  401.7 4.5 shard_map.254
  438.7 12.7 %collective-permute-done.65 = f32[256,1408]{1,0:T(8,128)} collective-permute-done((f32[256,1408]{1,0:T(8,128)}, f32[256,1408]{1,0:T(8,128)}, u32[]{:S(2)}, u32[]{:S(2)}) %collective-permute-start.65) | collective-permute-done | bytes 1441824 | tf_op jit(solution)/shard_map/ppermute | solution.py:426
  453.3 9.3 %collective-permute-done.61 = f32[256,512]{1,0:T(8,128)} collective-permute-done((f32[256,512]{1,0:T(8,128)}, f32[256,512]{1,0:T(8,128)}, u32[]{:S(2)}, u32[]{:S(2)}) %collective-permute-start.61) | collective-permute-done | bytes 524320 | tf_op jit(solution)/shard_map/ppermute | solution.py:426
  464.1 9.8 %collective-permute-done.57 = f32[256,512]{1,0:T(8,128)} collective-permute-done((f32[256,512]{1,0:T(8,128)S(1)}, f32[256,512]{1,0:T(8,128)}, u32[]{:S(2)}, u32[]{:S(2)}) %collective-permute-start.57) | collective-permute-done | bytes 524320 | tf_op jit(solution)/shard_map/ppermute | solution.py:426
  476.6 8.4 %collective-permute-done.53 = f32[256,512]{1,0:T(8,128)S(1)} collective-permute-done((f32[256,512]{1,0:T(8,128)S(1)}, f32[256,512]{1,0:T(8,128)S(1)}, u32[]{:S(2)}, u32[]{:S(2)}) %collective-permute-start.53) | collective-permute-done | bytes 524320 | tf_op jit(solution)/shard_map/ppermute | solution.py:426
  486.7 9.6 %collective-permute-done.49 = f32[256,512]{1,0:T(8,128)S(1)} collective-permute-done((f32[256,512]{1,0:T(8,128)S(1)}, f32[256,512]{1,0:T(8,128)S(1)}, u32[]{:S(2)}, u32[]{:S(2)}) %collective-permute-start.49) | collective-permute-done | bytes 524320 | tf_op jit(solution)/shard_map/ppermute | solution.py:426
  497.9 8.7 %collective-permute-done.45 = f32[256,512]{1,0:T(8,128)S(1)} collective-permute-done((f32[256,512]{1,0:T(8,128)S(1)}, f32[256,512]{1,0:T(8,128)S(1)}, u32[]{:S(2)}, u32[]{:S(2)}) %collective-permute-start.45) | collective-permute-done | bytes 524320 | tf_op jit(solution)/shard_map/ppermute | solution.py:426
  508.3 20.0 %collective-permute-done.62 = f32[128,512]{1,0:T(8,128)S(1)} collective-permute-done((f32[128,512]{1,0:T(8,128)S(1)}, f32[128,512]{1,0:T(8,128)S(1)}, u32[]{:S(2)}, u32[]{:S(2)}) %collective-permute-start.62) | collective-permute-done | bytes 262176 | tf_op jit(solution)/shard_map/ppermute | solution.py:426
  528.3 5.6 collective-permute-done.58
  533.9 5.6 collective-permute-done.54
  539.6 7.0 %collective-permute-done.50 = f32[128,512]{1,0:T(8,128)S(1)} collective-permute-done((f32[128,512]{1,0:T(8,128)S(1)}, f32[128,512]{1,0:T(8,128)S(1)}, u32[]{:S(2)}, u32[]{:S(2)}) %collective-permute-start.50) | collective-permute-done | bytes 262176 | tf_op jit(solution)/shard_map/ppermute | solution.py:426
  550.1 8.7 %collective-permute-done.63 = f32[64,512]{1,0:T(8,128)S(1)} collective-permute-done((f32[64,512]{1,0:T(8,128)S(1)}, f32[64,512]{1,0:T(8,128)S(1)}, u32[]{:S(2)}, u32[]{:S(2)}) %collective-permute-start.63) | collective-permute-done | bytes 131104 | tf_op jit(solution)/shard_map/ppermute | solution.py:426
  559.5 7.7 %collective-permute-done.59 = f32[64,512]{1,0:T(8,128)S(1)} collective-permute-done((f32[64,512]{1,0:T(8,128)S(1)}, f32[64,512]{1,0:T(8,128)S(1)}, u32[]{:S(2)}, u32[]{:S(2)}) %collective-permute-start.59) | collective-permute-done | bytes 131104 | tf_op jit(solution)/shard_map/ppermute | solution.py:426
  580.5 4.0 collective-permute-done.75
  585.4 14.7 %collective-permute-done.71 = f32[64,1408]{1,0:T(8,128)S(1)} collective-permute-done((f32[64,1408]{1,0:T(8,128)S(1)}, f32[64,1408]{1,0:T(8,128)S(1)}, u32[]{:S(2)}, u32[]{:S(2)}) %collective-permute-start.71) | collective-permute-done | bytes 360480 | tf_op jit(solution)/shard_map/ppermute | solution.py:426
  600.8 6.8 %collective-permute-done.67 = f32[64,1408]{1,0:T(8,128)S(1)} collective-permute-done((f32[64,1408]{1,0:T(8,128)S(1)}, f32[64,1408]{1,0:T(8,128)S(1)}, u32[]{:S(2)}, u32[]{:S(2)}) %collective-permute-start.67) | collective-permute-done | bytes 360480 | tf_op jit(solution)/shard_map/ppermute | solution.py:426
  (349 shorter events, 182.3 us)
Async XLA Ops:
  2.7 65.3 %collective-permute-start.8 = (f32[256,512]{1,0:T(8,128)}, f32[256,512]{1,0:T(8,128)S(1)}, u32[]{:S(2)}, u32[]{:S(2)}) collective-permute-start(f32[256,512]{1,0:T(8,128)} %maximum_convert_fusion.4), channel_id=1, source_target_pairs={{0,1},{1,0},{2,3},{3,2},{4,5},{5,4},{6,7},{7,6},{8,9},{9,8},{10,11... | collective-permute-start | bytes 1572872 | tf_op jit(solution)/shard_map/ppermute | solution.py:430
  6.5 62.9 %collective-permute-start.14 = (f32[256,512]{1,0:T(8,128)}, f32[256,512]{1,0:T(8,128)S(1)}, u32[]{:S(2)}, u32[]{:S(2)}) collective-permute-start(f32[256,512]{1,0:T(8,128)} %maximum_convert_fusion.5), channel_id=1, source_target_pairs={{0,1},{1,0},{2,3},{3,2},{4,5},{5,4},{6,7},{7,6},{8,9},{9,8},{10,11... | collective-permute-start | bytes 1572872 | tf_op jit(solution)/shard_map/ppermute | solution.py:430
  8.6 62.5 %collective-permute-start = (f32[256,512]{1,0:T(8,128)}, f32[256,512]{1,0:T(8,128)}, u32[]{:S(2)}, u32[]{:S(2)}) collective-permute-start(f32[256,512]{1,0:T(8,128)} %maximum_convert_fusion.2), channel_id=1, source_target_pairs={{0,1},{1,0},{2,3},{3,2},{4,5},{5,4},{6,7},{7,6},{8,9},{9,8},{10,11... | collective-permute-start | bytes 1572872 | tf_op jit(solution)/shard_map/ppermute | solution.py:430
  11.4 59.6 %collective-permute-start.6 = (f32[256,512]{1,0:T(8,128)}, f32[256,512]{1,0:T(8,128)}, u32[]{:S(2)}, u32[]{:S(2)}) collective-permute-start(f32[256,512]{1,0:T(8,128)} %maximum_convert_fusion.3), channel_id=1, source_target_pairs={{0,1},{1,0},{2,3},{3,2},{4,5},{5,4},{6,7},{7,6},{8,9},{9,8},{10,11... | collective-permute-start | bytes 1572872 | tf_op jit(solution)/shard_map/ppermute | solution.py:430
  13.3 43.9 %collective-permute-start.16 = (f32[64,1024]{1,0:T(8,128)}, f32[64,1024]{1,0:T(8,128)S(1)}, u32[]{:S(2)}, u32[]{:S(2)}) collective-permute-start(f32[64,1024]{1,0:T(8,128)} %get-tuple-element.109), channel_id=1, source_target_pairs={{0,1},{1,0},{2,3},{3,2},{4,5},{5,4},{6,7},{7,6},{8,9},{9,8},{10,11... | collective-permute-start | bytes 786440 | tf_op jit(solution)/shard_map/ppermute | solution.py:430
  64.6 16.5 %collective-permute-start.32 = (f32[176,1024]{1,0:T(8,128)S(1)}, f32[176,1024]{1,0:T(8,128)}, u32[]{:S(2)}, u32[]{:S(2)}) collective-permute-start(f32[176,1024]{1,0:T(8,128)S(1)} %get-tuple-element.93), channel_id=1, source_target_pairs={{0,1},{1,0},{2,3},{3,2},{4,5},{5,4},{6,7},{7,6},{8,9},{9,8},{10,11... | collective-permute-start | bytes 2162696 | tf_op jit(solution)/shard_map/ppermute | solution.py:430
  76.1 14.9 %collective-permute-start.10 = (f32[256,512]{1,0:T(8,128)S(1)}, f32[256,512]{1,0:T(8,128)}, u32[]{:S(2)}, u32[]{:S(2)}) collective-permute-start(f32[256,512]{1,0:T(8,128)S(1)} %collective-permute-done.8.refs_0_), channel_id=1, source_target_pairs={{0,4},{2,6},{4,0},{6,2},{8,12},{10,14},{12,8},{14,10},{16,20},{18,... | collective-permute-start | bytes 1572872 | tf_op jit(solution)/shard_map/ppermute | solution.py:426
  83.4 17.9 %collective-permute-start.2 = (f32[256,512]{1,0:T(8,128)}, f32[256,512]{1,0:T(8,128)}, u32[]{:S(2)}, u32[]{:S(2)}) collective-permute-start(f32[256,512]{1,0:T(8,128)} %collective-permute-done.refs_0_), channel_id=1, source_target_pairs={{0,4},{2,6},{4,0},{6,2},{8,12},{10,14},{12,8},{14,10},{16,20},{18,... | collective-permute-start | bytes 1572872 | tf_op jit(solution)/shard_map/ppermute | solution.py:426
  93.9 15.7 %collective-permute-start.11 = (f32[256,512]{1,0:T(8,128)}, f32[256,512]{1,0:T(8,128)}, u32[]{:S(2)}, u32[]{:S(2)}) collective-permute-start(f32[256,512]{1,0:T(8,128)} %collective-permute-done.10.refs_2_), channel_id=1, source_target_pairs={{0,2},{2,0},{4,6},{6,4},{8,10},{10,8},{12,14},{14,12},{16,18},{18,... | collective-permute-start | bytes 1572872 | tf_op jit(solution)/shard_map/ppermute | solution.py:426
  101.3 79.4 %collective-permute-start.24 = (f32[256,1408]{1,0:T(8,128)}, f32[256,1408]{1,0:T(8,128)S(1)}, u32[]{:S(2)}, u32[]{:S(2)}) collective-permute-start(f32[256,1408]{1,0:T(8,128)} %maximum_convert_fusion), channel_id=1, source_target_pairs={{0,1},{1,0},{2,3},{3,2},{4,5},{5,4},{6,7},{7,6},{8,9},{9,8},{10,11... | collective-permute-start | bytes 4325384 | tf_op jit(solution)/shard_map/ppermute | solution.py:430
  103.5 77.8 %collective-permute-start.30 = (f32[256,1408]{1,0:T(8,128)}, f32[256,1408]{1,0:T(8,128)S(1)}, u32[]{:S(2)}, u32[]{:S(2)}) collective-permute-start(f32[256,1408]{1,0:T(8,128)} %maximum_convert_fusion.1), channel_id=1, source_target_pairs={{0,1},{1,0},{2,3},{3,2},{4,5},{5,4},{6,7},{7,6},{8,9},{9,8},{10,11... | collective-permute-start | bytes 4325384 | tf_op jit(solution)/shard_map/ppermute | solution.py:430
  109.6 29.3 %collective-permute-start.5 = (f32[256,512]{1,0:T(8,128)}, f32[256,512]{1,0:T(8,128)S(1)}, u32[]{:S(2)}, u32[]{:S(2)}) collective-permute-start(f32[256,512]{1,0:T(8,128)} %collective-permute-done.4.refs_4_), channel_id=1, source_target_pairs={{0,2},{2,0},{4,6},{6,4},{8,10},{10,8},{12,14},{14,12},{16,18},{18,... | collective-permute-start | bytes 1572872 | tf_op jit(solution)/shard_map/ppermute | solution.py:426
  113.1 67.7 %collective-permute-start.38 = (f32[176,1024]{1,0:T(8,128)}, f32[176,1024]{1,0:T(8,128)}, u32[]{:S(2)}, u32[]{:S(2)}) collective-permute-start(f32[176,1024]{1,0:T(8,128)} %get-tuple-element.92), channel_id=1, source_target_pairs={{0,1},{1,0},{2,3},{3,2},{4,5},{5,4},{6,7},{7,6},{8,9},{9,8},{10,11... | collective-permute-start | bytes 2162696 | tf_op jit(solution)/shard_map/ppermute | solution.py:430
  114.7 67.1 %collective-permute-start.34 = (f32[176,1024]{1,0:T(8,128)}, f32[176,1024]{1,0:T(8,128)}, u32[]{:S(2)}, u32[]{:S(2)}) collective-permute-start(f32[176,1024]{1,0:T(8,128)} %collective-permute-done.32.refs_0_), channel_id=1, source_target_pairs={{0,4},{2,6},{4,0},{6,2},{8,12},{10,14},{12,8},{14,10},{16,20},{18,... | collective-permute-start | bytes 2162696 | tf_op jit(solution)/shard_map/ppermute | solution.py:426
  138.9 78.3 %collective-permute-start.36 = (f32[176,1024]{1,0:T(8,128)}, f32[176,1024]{1,0:T(8,128)}, u32[]{:S(2)}, u32[]{:S(2)}) collective-permute-start(f32[176,1024]{1,0:T(8,128)} %collective-permute-done.32.refs_0_), channel_id=1, source_target_pairs={{0,8},{2,10},{4,12},{6,14},{8,0},{10,2},{12,4},{14,6},{16,24},{18,... | collective-permute-start | bytes 2162696 | tf_op jit(solution)/shard_map/ppermute | solution.py:426
  180.7 36.5 %collective-permute-start.33 = (f32[176,1024]{1,0:T(8,128)}, f32[176,1024]{1,0:T(8,128)}, u32[]{:S(2)}, u32[]{:S(2)}) collective-permute-start(f32[176,1024]{1,0:T(8,128)} %collective-permute-done.32.refs_0_), channel_id=1, source_target_pairs={{0,2},{2,0},{4,6},{6,4},{8,10},{10,8},{12,14},{14,12},{16,18},{18,... | collective-permute-start | bytes 2162696 | tf_op jit(solution)/shard_map/ppermute | solution.py:426
  180.7 37.0 %collective-permute-start.39 = (f32[176,1024]{1,0:T(8,128)}, f32[176,1024]{1,0:T(8,128)}, u32[]{:S(2)}, u32[]{:S(2)}) collective-permute-start(f32[176,1024]{1,0:T(8,128)} %collective-permute-done.38.refs_6_), channel_id=1, source_target_pairs={{0,2},{2,0},{4,6},{6,4},{8,10},{10,8},{12,14},{14,12},{16,18},{18,... | collective-permute-start | bytes 2162696 | tf_op jit(solution)/shard_map/ppermute | solution.py:426
  181.3 36.6 %collective-permute-start.26 = (f32[256,1408]{1,0:T(8,128)S(1)}, f32[256,1408]{1,0:T(8,128)}, u32[]{:S(2)}, u32[]{:S(2)}) collective-permute-start(f32[256,1408]{1,0:T(8,128)S(1)} %collective-permute-done.24.refs_0_), channel_id=1, source_target_pairs={{0,4},{2,6},{4,0},{6,2},{8,12},{10,14},{12,8},{14,10},{16,20},{18,... | collective-permute-start | bytes 4325384 | tf_op jit(solution)/shard_map/ppermute | solution.py:426
  181.8 36.5 %collective-permute-start.28 = (f32[256,1408]{1,0:T(8,128)S(1)}, f32[256,1408]{1,0:T(8,128)}, u32[]{:S(2)}, u32[]{:S(2)}) collective-permute-start(f32[256,1408]{1,0:T(8,128)S(1)} %collective-permute-done.24.refs_0_), channel_id=1, source_target_pairs={{0,8},{2,10},{4,12},{6,14},{8,0},{10,2},{12,4},{14,6},{16,24},{18,... | collective-permute-start | bytes 4325384 | tf_op jit(solution)/shard_map/ppermute | solution.py:426
  217.2 30.4 %collective-permute-start.25 = (f32[256,1408]{1,0:T(8,128)S(1)}, f32[256,1408]{1,0:T(8,128)S(1)}, u32[]{:S(2)}, u32[]{:S(2)}) collective-permute-start(f32[256,1408]{1,0:T(8,128)S(1)} %collective-permute-done.24.refs_0_), channel_id=1, source_target_pairs={{0,2},{2,0},{4,6},{6,4},{8,10},{10,8},{12,14},{14,12},{16,18},{18,... | collective-permute-start | bytes 4325384 | tf_op jit(solution)/shard_map/ppermute | solution.py:426
  217.3 30.5 %collective-permute-start.31 = (f32[256,1408]{1,0:T(8,128)S(1)}, f32[256,1408]{1,0:T(8,128)S(1)}, u32[]{:S(2)}, u32[]{:S(2)}) collective-permute-start(f32[256,1408]{1,0:T(8,128)S(1)} %collective-permute-done.30.refs_6_), channel_id=1, source_target_pairs={{0,2},{2,0},{4,6},{6,4},{8,10},{10,8},{12,14},{14,12},{16,18},{18,... | collective-permute-start | bytes 4325384 | tf_op jit(solution)/shard_map/ppermute | solution.py:426
  217.9 30.2 %collective-permute-start.27 = (f32[256,1408]{1,0:T(8,128)}, f32[256,1408]{1,0:T(8,128)S(1)}, u32[]{:S(2)}, u32[]{:S(2)}) collective-permute-start(f32[256,1408]{1,0:T(8,128)} %collective-permute-done.26.refs_2_), channel_id=1, source_target_pairs={{0,2},{2,0},{4,6},{6,4},{8,10},{10,8},{12,14},{14,12},{16,18},{18,... | collective-permute-start | bytes 4325384 | tf_op jit(solution)/shard_map/ppermute | solution.py:426
  218.3 29.8 %collective-permute-start.29 = (f32[256,1408]{1,0:T(8,128)}, f32[256,1408]{1,0:T(8,128)}, u32[]{:S(2)}, u32[]{:S(2)}) collective-permute-start(f32[256,1408]{1,0:T(8,128)} %collective-permute-done.28.refs_4_), channel_id=1, source_target_pairs={{0,2},{2,0},{4,6},{6,4},{8,10},{10,8},{12,14},{14,12},{16,18},{18,... | collective-permute-start | bytes 4325384 | tf_op jit(solution)/shard_map/ppermute | solution.py:426
  223.8 17.6 %collective-permute-start.37 = (f32[176,1024]{1,0:T(8,128)}, f32[176,1024]{1,0:T(8,128)}, u32[]{:S(2)}, u32[]{:S(2)}) collective-permute-start(f32[176,1024]{1,0:T(8,128)} %collective-permute-done.36.refs_4_), channel_id=1, source_target_pairs={{0,2},{2,0},{4,6},{6,4},{8,10},{10,8},{12,14},{14,12},{16,18},{18,... | collective-permute-start | bytes 2162696 | tf_op jit(solution)/shard_map/ppermute | solution.py:426
  241.4 122.0 %collective-permute-start.72 = (f32[512,1408]{1,0:T(8,128)}, f32[512,1408]{1,0:T(8,128)}, u32[]{:S(2)}, u32[]{:S(2)}) collective-permute-start(f32[512,1408]{1,0:T(8,128)} %shard_map.259), channel_id=1, source_target_pairs={{0,2},{2,0},{4,6},{6,4},{8,10},{10,8},{12,14},{14,12},{16,18},{18,... | collective-permute-start | bytes 8650760 | tf_op jit(solution)/shard_map/ppermute | solution.py:426
  247.6 126.4 %collective-permute-start.68 = (f32[512,1408]{1,0:T(8,128)}, f32[512,1408]{1,0:T(8,128)}, u32[]{:S(2)}, u32[]{:S(2)}) collective-permute-start(f32[512,1408]{1,0:T(8,128)} %shard_map.256), channel_id=1, source_target_pairs={{0,2},{2,0},{4,6},{6,4},{8,10},{10,8},{12,14},{14,12},{16,18},{18,... | collective-permute-start | bytes 8650760 | tf_op jit(solution)/shard_map/ppermute | solution.py:426
  247.8 129.3 %collective-permute-start.64 = (f32[512,1408]{1,0:T(8,128)}, f32[512,1408]{1,0:T(8,128)}, u32[]{:S(2)}, u32[]{:S(2)}) collective-permute-start(f32[512,1408]{1,0:T(8,128)} %shard_map.253), channel_id=1, source_target_pairs={{0,2},{2,0},{4,6},{6,4},{8,10},{10,8},{12,14},{14,12},{16,18},{18,... | collective-permute-start | bytes 8650760 | tf_op jit(solution)/shard_map/ppermute | solution.py:426
  358.3 22.4 %collective-permute-start.60 = (f32[512,512]{1,0:T(8,128)}, f32[512,512]{1,0:T(8,128)S(1)}, u32[]{:S(2)}, u32[]{:S(2)}) collective-permute-start(f32[512,512]{1,0:T(8,128)} %shard_map.250), channel_id=1, source_target_pairs={{0,2},{2,0},{4,6},{6,4},{8,10},{10,8},{12,14},{14,12},{16,18},{18,... | collective-permute-start | bytes 3145736 | tf_op jit(solution)/shard_map/ppermute | solution.py:426
  363.1 22.5 %collective-permute-start.56 = (f32[512,512]{1,0:T(8,128)}, f32[512,512]{1,0:T(8,128)S(1)}, u32[]{:S(2)}, u32[]{:S(2)}) collective-permute-start(f32[512,512]{1,0:T(8,128)} %shard_map.247), channel_id=1, source_target_pairs={{0,2},{2,0},{4,6},{6,4},{8,10},{10,8},{12,14},{14,12},{16,18},{18,... | collective-permute-start | bytes 3145736 | tf_op jit(solution)/shard_map/ppermute | solution.py:426
  370.5 65.6 %collective-permute-start.73 = (f32[256,1408]{1,0:T(8,128)}, f32[256,1408]{1,0:T(8,128)S(1)}, u32[]{:S(2)}, u32[]{:S(2)}) collective-permute-start(f32[256,1408]{1,0:T(8,128)} %shard_map.261), channel_id=1, source_target_pairs={{0,8},{2,10},{4,12},{6,14},{8,0},{10,2},{12,4},{14,6},{16,24},{18,... | collective-permute-start | bytes 4325384 | tf_op jit(solution)/shard_map/ppermute | solution.py:426
  374.0 21.6 %collective-permute-start.52 = (f32[512,512]{1,0:T(8,128)}, f32[512,512]{1,0:T(8,128)S(1)}, u32[]{:S(2)}, u32[]{:S(2)}) collective-permute-start(f32[512,512]{1,0:T(8,128)} %shard_map.244), channel_id=1, source_target_pairs={{0,2},{2,0},{4,6},{6,4},{8,10},{10,8},{12,14},{14,12},{16,18},{18,... | collective-permute-start | bytes 3145736 | tf_op jit(solution)/shard_map/ppermute | solution.py:426
  377.2 45.6 %collective-permute-start.48 = (f32[512,512]{1,0:T(8,128)}, f32[512,512]{1,0:T(8,128)S(1)}, u32[]{:S(2)}, u32[]{:S(2)}) collective-permute-start(f32[512,512]{1,0:T(8,128)} %shard_map.241), channel_id=1, source_target_pairs={{0,2},{2,0},{4,6},{6,4},{8,10},{10,8},{12,14},{14,12},{16,18},{18,... | collective-permute-start | bytes 3145736 | tf_op jit(solution)/shard_map/ppermute | solution.py:426
  380.7 48.6 %collective-permute-start.44 = (f32[512,512]{1,0:T(8,128)}, f32[512,512]{1,0:T(8,128)S(1)}, u32[]{:S(2)}, u32[]{:S(2)}) collective-permute-start(f32[512,512]{1,0:T(8,128)} %shard_map.238), channel_id=1, source_target_pairs={{0,2},{2,0},{4,6},{6,4},{8,10},{10,8},{12,14},{14,12},{16,18},{18,... | collective-permute-start | bytes 3145736 | tf_op jit(solution)/shard_map/ppermute | solution.py:426
  385.7 51.7 %collective-permute-start.69 = (f32[256,1408]{1,0:T(8,128)}, f32[256,1408]{1,0:T(8,128)S(1)}, u32[]{:S(2)}, u32[]{:S(2)}) collective-permute-start(f32[256,1408]{1,0:T(8,128)} %shard_map.258), channel_id=1, source_target_pairs={{0,4},{2,6},{4,0},{6,2},{8,12},{10,14},{12,8},{14,10},{16,20},{18,... | collective-permute-start | bytes 4325384 | tf_op jit(solution)/shard_map/ppermute | solution.py:426
  395.6 55.7 %collective-permute-start.65 = (f32[256,1408]{1,0:T(8,128)}, f32[256,1408]{1,0:T(8,128)}, u32[]{:S(2)}, u32[]{:S(2)}) collective-permute-start(f32[256,1408]{1,0:T(8,128)} %shard_map.255), channel_id=1, source_target_pairs={{0,4},{2,6},{4,0},{6,2},{8,12},{10,14},{12,8},{14,10},{16,20},{18,... | collective-permute-start | bytes 4325384 | tf_op jit(solution)/shard_map/ppermute | solution.py:426
  422.7 39.9 %collective-permute-start.61 = (f32[256,512]{1,0:T(8,128)}, f32[256,512]{1,0:T(8,128)}, u32[]{:S(2)}, u32[]{:S(2)}) collective-permute-start(f32[256,512]{1,0:T(8,128)} %shard_map.252), channel_id=1, source_target_pairs={{0,4},{2,6},{4,0},{6,2},{8,12},{10,14},{12,8},{14,10},{16,20},{18,... | collective-permute-start | bytes 1572872 | tf_op jit(solution)/shard_map/ppermute | solution.py:426
  429.3 44.6 %collective-permute-start.57 = (f32[256,512]{1,0:T(8,128)S(1)}, f32[256,512]{1,0:T(8,128)}, u32[]{:S(2)}, u32[]{:S(2)}) collective-permute-start(f32[256,512]{1,0:T(8,128)S(1)} %copy-done.54), channel_id=1, source_target_pairs={{0,4},{2,6},{4,0},{6,2},{8,12},{10,14},{12,8},{14,10},{16,20},{18,... | collective-permute-start | bytes 1572872 | tf_op jit(solution)/shard_map/ppermute | solution.py:426
  436.1 48.9 %collective-permute-start.53 = (f32[256,512]{1,0:T(8,128)S(1)}, f32[256,512]{1,0:T(8,128)S(1)}, u32[]{:S(2)}, u32[]{:S(2)}) collective-permute-start(f32[256,512]{1,0:T(8,128)S(1)} %copy-done.53), channel_id=1, source_target_pairs={{0,4},{2,6},{4,0},{6,2},{8,12},{10,14},{12,8},{14,10},{16,20},{18,... | collective-permute-start | bytes 1572872 | tf_op jit(solution)/shard_map/ppermute | solution.py:426
  437.3 58.9 %collective-permute-start.49 = (f32[256,512]{1,0:T(8,128)S(1)}, f32[256,512]{1,0:T(8,128)S(1)}, u32[]{:S(2)}, u32[]{:S(2)}) collective-permute-start(f32[256,512]{1,0:T(8,128)S(1)} %copy-done.52), channel_id=1, source_target_pairs={{0,4},{2,6},{4,0},{6,2},{8,12},{10,14},{12,8},{14,10},{16,20},{18,... | collective-permute-start | bytes 1572872 | tf_op jit(solution)/shard_map/ppermute | solution.py:426
  451.4 55.2 %collective-permute-start.45 = (f32[256,512]{1,0:T(8,128)S(1)}, f32[256,512]{1,0:T(8,128)S(1)}, u32[]{:S(2)}, u32[]{:S(2)}) collective-permute-start(f32[256,512]{1,0:T(8,128)S(1)} %copy-done.51), channel_id=1, source_target_pairs={{0,4},{2,6},{4,0},{6,2},{8,12},{10,14},{12,8},{14,10},{16,20},{18,... | collective-permute-start | bytes 1572872 | tf_op jit(solution)/shard_map/ppermute | solution.py:426
  462.6 114.0 %collective-permute-start.74 = (f32[128,1408]{1,0:T(8,128)S(1)}, f32[128,1408]{1,0:T(8,128)S(1)}, u32[]{:S(2)}, u32[]{:S(2)}) collective-permute-start(f32[128,1408]{1,0:T(8,128)S(1)} %get-tuple-element.87), channel_id=1, source_target_pairs={{0,16},{2,18},{4,20},{6,22},{8,24},{10,26},{12,28},{14,30},{16,0},... | collective-permute-start | bytes 2162696 | tf_op jit(solution)/shard_map/ppermute | solution.py:426
  473.8 103.5 %collective-permute-start.70 = (f32[128,1408]{1,0:T(8,128)S(1)}, f32[128,1408]{1,0:T(8,128)S(1)}, u32[]{:S(2)}, u32[]{:S(2)}) collective-permute-start(f32[128,1408]{1,0:T(8,128)S(1)} %get-tuple-element.89), channel_id=1, source_target_pairs={{0,8},{2,10},{4,12},{6,14},{8,0},{10,2},{12,4},{14,6},{16,24},{18,... | collective-permute-start | bytes 2162696 | tf_op jit(solution)/shard_map/ppermute | solution.py:426
  485.0 93.3 %collective-permute-start.66 = (f32[128,1408]{1,0:T(8,128)S(1)}, f32[128,1408]{1,0:T(8,128)S(1)}, u32[]{:S(2)}, u32[]{:S(2)}) collective-permute-start(f32[128,1408]{1,0:T(8,128)S(1)} %get-tuple-element.91), channel_id=1, source_target_pairs={{0,8},{2,10},{4,12},{6,14},{8,0},{10,2},{12,4},{14,6},{16,24},{18,... | collective-permute-start | bytes 2162696 | tf_op jit(solution)/shard_map/ppermute | solution.py:426
  496.2 32.1 %collective-permute-start.62 = (f32[128,512]{1,0:T(8,128)S(1)}, f32[128,512]{1,0:T(8,128)S(1)}, u32[]{:S(2)}, u32[]{:S(2)}) collective-permute-start(f32[128,512]{1,0:T(8,128)S(1)} %get-tuple-element.99), channel_id=1, source_target_pairs={{0,8},{2,10},{4,12},{6,14},{8,0},{10,2},{12,4},{14,6},{16,24},{18,... | collective-permute-start | bytes 786440 | tf_op jit(solution)/shard_map/ppermute | solution.py:426
  506.6 27.3 %collective-permute-start.58 = (f32[128,512]{1,0:T(8,128)S(1)}, f32[128,512]{1,0:T(8,128)S(1)}, u32[]{:S(2)}, u32[]{:S(2)}) collective-permute-start(f32[128,512]{1,0:T(8,128)S(1)} %get-tuple-element.101), channel_id=1, source_target_pairs={{0,8},{2,10},{4,12},{6,14},{8,0},{10,2},{12,4},{14,6},{16,24},{18,... | collective-permute-start | bytes 786440 | tf_op jit(solution)/shard_map/ppermute | solution.py:426
  549.6 17.7 %collective-permute-start.59 = (f32[64,512]{1,0:T(8,128)S(1)}, f32[64,512]{1,0:T(8,128)S(1)}, u32[]{:S(2)}, u32[]{:S(2)}) collective-permute-start(f32[64,512]{1,0:T(8,128)S(1)} %slice_add_fusion.24), channel_id=1, source_target_pairs={{0,16},{2,18},{4,20},{6,22},{8,24},{10,26},{12,28},{14,30},{16,0},... | collective-permute-start | bytes 393224 | tf_op jit(solution)/shard_map/ppermute | solution.py:426
  577.4 22.6 %collective-permute-start.71 = (f32[64,1408]{1,0:T(8,128)S(1)}, f32[64,1408]{1,0:T(8,128)S(1)}, u32[]{:S(2)}, u32[]{:S(2)}) collective-permute-start(f32[64,1408]{1,0:T(8,128)S(1)} %slice_add_fusion.8), channel_id=1, source_target_pairs={{0,16},{2,18},{4,20},{6,22},{8,24},{10,26},{12,28},{14,30},{16,0},... | collective-permute-start | bytes 1081352 | tf_op jit(solution)/shard_map/ppermute | solution.py:426
  578.3 29.3 %collective-permute-start.67 = (f32[64,1408]{1,0:T(8,128)S(1)}, f32[64,1408]{1,0:T(8,128)S(1)}, u32[]{:S(2)}, u32[]{:S(2)}) collective-permute-start(f32[64,1408]{1,0:T(8,128)S(1)} %slice_add_fusion.10), channel_id=1, source_target_pairs={{0,16},{2,18},{4,20},{6,22},{8,24},{10,26},{12,28},{14,30},{16,0},... | collective-permute-start | bytes 1081352 | tf_op jit(solution)/shard_map/ppermute | solution.py:426
  (87 other events, 694.0 us)
